TPU v7x, 256 devices: a whole 4x4x8 slice. The times are simulated.
256 devices in a mesh: seq: 64 (over z, x, core), head: 4 (over y).
Axes of the slice: x: 4, y: 4, z: 8, core: 2. Of those that a mesh axis runs over, the one named last changes fastest.
Arguments:
- frames: bfloat16 [131072, 1024], P('seq'), may hold values from -16 to 16
- text_states: bfloat16 [16384, 1024], P('seq'), may hold values from -48 to 48
- durations: int32 [64, 256], P('seq'), may hold values from 1 to 32, 2048 in all within a row
- w_query: bfloat16 [1024, 1024], P(None, 'head'), may hold values from -0.1875 to 0.1875
- w_key: bfloat16 [1024, 1024], P(None, 'head'), may hold values from -0.1875 to 0.1875
- w_value: bfloat16 [1024, 1024], P(None, 'head'), may hold values from -0.1875 to 0.1875
- w_out: bfloat16 [1024, 1024], P('head'), may hold values from -0.1875 to 0.1875
- cotangent: bfloat16 [131072, 1024], P('seq'), may hold values from -16 to 16
Outputs:
- layer_out: bfloat16 [131072, 1024], P(('seq', 'head'))
- frames_grad: bfloat16 [131072, 1024], P(('seq', 'head'))
- text_grad: bfloat16 [16384, 1024], P(('seq', 'head'))
- query_wgrad: float32 [1024, 1024], P('seq', 'head')
- key_wgrad: float32 [1024, 1024], P('seq', 'head')
- value_wgrad: float32 [1024, 1024], P('seq', 'head')
- out_wgrad: float32 [1024, 1024], P('head', 'seq')
Inputs may be any that keep to these rules, and one draw needn't show every extreme that they name: `durations`: each row sums to 2048 and its largest entry is 32.
All inputs are finite; a program needn't handle non-finite values.
Results may differ from a plain program's by a relative error of at most 0.034.
The roundings to bfloat16 on the way count: a program that leaves them out, or rounds other values in their place, can miss the bound.
Values may be sent and summed in bfloat16 or wider, within the bound.
A program may use at most 128 MiB of HBM per device.

v0:
```python
import jax
import jax.numpy as jnp
from jax import lax
from jax.sharding import PartitionSpec as P

HEAD_DIM = 64
WINDOW = 32


def extended(block, sides, width):
    for axis, dim in sides:
        count = lax.axis_size(axis)
        forward = [(i, i + 1) for i in range(count - 1)]
        backward = [(target, source) for source, target in forward]
        low = lax.ppermute(
            lax.slice_in_dim(block, block.shape[dim] - width, None, axis=dim), axis, forward
        )
        high = lax.ppermute(lax.slice_in_dim(block, 0, width, axis=dim), axis, backward)
        block = jnp.concatenate([low, block, high], axis=dim)
    return block


def shifted_2(value, axis, by):
    devices = lax.axis_size(axis)
    pairs = [(i, i + by) for i in range(devices) if 0 <= i + by < devices]
    return lax.ppermute(value, axis, pairs)


def band_mask(lengths_row, shard_index, frame_rows, text_rows, total_text):
    ends = jnp.cumsum(lengths_row, dtype=jnp.int32)
    positions = jnp.arange(frame_rows, dtype=jnp.int32)
    token_of = jnp.sum(
        (ends[None, :] <= positions[:, None]).astype(jnp.int32), axis=1, dtype=jnp.int32
    )
    ext_index = jnp.arange(text_rows + 2 * WINDOW, dtype=jnp.int32)
    global_index = shard_index * text_rows - WINDOW + ext_index
    near = jnp.abs(ext_index[None, :] - WINDOW - token_of[:, None]) <= WINDOW
    inside = (global_index >= 0) & (global_index < total_text)
    return near & inside[None, :]


def on_device(frames, text_states, durations, w_query, w_key, w_value, w_out, cotangent):
    frame_rows = frames.shape[0]
    text_rows = text_states.shape[0]
    local_width = w_query.shape[1]
    head_count = local_width // HEAD_DIM
    ext_rows = text_rows + 2 * WINDOW
    attn_scale = HEAD_DIM ** (-0.5)
    shard_index = lax.axis_index("seq")
    query = jnp.dot(frames, w_query, preferred_element_type=jnp.float32).astype(jnp.bfloat16)
    keys = jnp.dot(text_states, w_key, preferred_element_type=jnp.float32).astype(jnp.bfloat16)
    values = jnp.dot(text_states, w_value, preferred_element_type=jnp.float32).astype(jnp.bfloat16)
    joined = jnp.concatenate([keys, values], axis=1)
    padded = extended(joined, (("seq", 0),), WINDOW)
    allowed = band_mask(
        durations[0], shard_index, frame_rows, text_rows, text_rows * lax.axis_size("seq")
    )
    query_heads = query.reshape(frame_rows, head_count, HEAD_DIM)
    key_heads = padded[:, :local_width].reshape(ext_rows, head_count, HEAD_DIM)
    val_heads = padded[:, local_width:].reshape(ext_rows, head_count, HEAD_DIM)
    scores = (
        jnp.einsum("fhd,khd->hfk", query_heads, key_heads, preferred_element_type=jnp.float32)
        * attn_scale
    )
    scores = jnp.where(allowed[None], scores, -jnp.inf)
    largest = jnp.max(scores, axis=-1, keepdims=True)
    shifted = jnp.exp(scores - largest)
    prob = shifted / jnp.sum(shifted, axis=-1, keepdims=True)
    prob_b = prob.astype(jnp.bfloat16)
    att_heads = jnp.einsum(
        "hfk,khd->fhd", prob_b, val_heads, preferred_element_type=jnp.float32
    ).astype(jnp.bfloat16)
    attended = att_heads.reshape(frame_rows, local_width)
    part_rows = attended
    layer_out = lax.psum_scatter(
        jnp.dot(part_rows, w_out, preferred_element_type=jnp.float32).astype(jnp.bfloat16),
        "head",
        scatter_dimension=0,
        tiled=True,
    )
    upstream = lax.dot_general(
        cotangent, w_out, (((1,), (1,)), ((), ())), preferred_element_type=jnp.float32
    ).astype(jnp.bfloat16)
    up_heads = upstream.reshape(frame_rows, head_count, HEAD_DIM)
    dprob = jnp.einsum("fhd,khd->hfk", up_heads, val_heads, preferred_element_type=jnp.float32)
    delta = jnp.sum(up_heads.astype(jnp.float32) * att_heads.astype(jnp.float32), axis=2)
    dscore = (prob * (dprob - jnp.transpose(delta)[:, :, None]) * attn_scale).astype(jnp.bfloat16)
    dquery = (
        jnp.einsum("hfk,khd->fhd", dscore, key_heads, preferred_element_type=jnp.float32)
        .astype(jnp.bfloat16)
        .reshape(frame_rows, local_width)
    )
    dkey = jnp.einsum(
        "hfk,fhd->khd", dscore, query_heads, preferred_element_type=jnp.float32
    ).reshape(ext_rows, local_width)
    dval = jnp.einsum("hfk,fhd->khd", prob_b, up_heads, preferred_element_type=jnp.float32).reshape(
        ext_rows, local_width
    )
    grads_ext = jnp.concatenate([dkey, dval], axis=1)
    from_above = shifted_2(grads_ext[:WINDOW].astype(jnp.bfloat16), "seq", -1).astype(jnp.float32)
    from_below = shifted_2(grads_ext[text_rows + WINDOW :].astype(jnp.bfloat16), "seq", 1).astype(
        jnp.float32
    )
    inner = grads_ext[WINDOW : WINDOW + text_rows]
    inner = inner + jnp.pad(from_below, ((0, text_rows - WINDOW), (0, 0)))
    inner = inner + jnp.pad(from_above, ((text_rows - WINDOW, 0), (0, 0)))
    kv_grad = inner.astype(jnp.bfloat16)
    part_rows = dquery
    frames_grad = lax.psum_scatter(
        lax.dot_general(
            part_rows, w_query, (((1,), (1,)), ((), ())), preferred_element_type=jnp.float32
        ).astype(jnp.bfloat16),
        "head",
        scatter_dimension=0,
        tiled=True,
    )
    text_weights = jnp.concatenate([w_key, w_value], axis=1)
    part_rows = kv_grad
    text_grad = lax.psum_scatter(
        lax.dot_general(
            part_rows, text_weights, (((1,), (1,)), ((), ())), preferred_element_type=jnp.float32
        ).astype(jnp.bfloat16),
        "head",
        scatter_dimension=0,
        tiled=True,
    )
    dims = (((0,), (0,)), ((), ()))
    query_term_w = lax.dot_general(frames, dquery, dims, preferred_element_type=jnp.float32)
    query_wgrad = lax.psum_scatter(query_term_w, "seq", scatter_dimension=0, tiled=True)
    key_term_w = lax.dot_general(
        text_states, kv_grad[:, :local_width], dims, preferred_element_type=jnp.float32
    )
    value_term_w = lax.dot_general(
        text_states, kv_grad[:, local_width:], dims, preferred_element_type=jnp.float32
    )
    key_wgrad, value_wgrad = (
        lax.psum_scatter(key_term_w, "seq", scatter_dimension=0, tiled=True),
        lax.psum_scatter(value_term_w, "seq", scatter_dimension=0, tiled=True),
    )
    out_term_w = lax.dot_general(attended, cotangent, dims, preferred_element_type=jnp.float32)
    out_wgrad = lax.psum_scatter(out_term_w, "seq", scatter_dimension=1, tiled=True)
    return (layer_out, frames_grad, text_grad, query_wgrad, key_wgrad, value_wgrad, out_wgrad)


def solution(mesh):
    placed = (
        P("seq", None),
        P("seq", None),
        P("seq", None),
        P(None, "head"),
        P(None, "head"),
        P(None, "head"),
        P("head", None),
        P("seq", None),
    )
    return jax.shard_map(
        on_device,
        mesh=mesh,
        in_specs=placed,
        out_specs=(
            P(("seq", "head"), None),
            P(("seq", "head"), None),
            P(("seq", "head"), None),
            P("seq", "head"),
            P("seq", "head"),
            P("seq", "head"),
            P("head", "seq"),
        ),
        check_vma=False,
    )
```

profile of v0, /device:TPU:1, one launch (start us, length us, event | category | flops | bytes accessed | tf_op | source)
XLA Modules:
  0.0 776.9 jit_solution(16187553390350785586)
XLA Ops:
  7.2 1.6 convolution_convert_fusion.8
  8.8 1.6 convolution_convert_fusion.7
  10.4 0.1 fusion.17
  10.5 4.5 collective-permute-start
  15.1 1.9 collective-permute-start.1
  17.0 1.0 reduce-window.9
  18.0 0.1 slice.39
  18.1 0.1 slice_reduce_fusion
  18.3 0.1 add_bitcast_fusion
  18.3 0.3 convert_reduce_fusion
  18.7 3.7 convolution_convert_fusion.4
  22.4 0.9 fusion.8
  23.3 2.3 convolution_convert_fusion.5
  25.6 0.2 pad_maximum_fusion.1
  25.9 9.2 %fusion.28 = (f32[4,2048]{1,0:T(4,128)S(1)}, f32[4,2048,320]{1,2,0:T(8,128)}) fusion(pred[2048,320]{0,1:T(8,128)(4,1)S(1)} %fusion.8, bf16[2048,4,64]{0,2,1:T(8,128)(2,1)} %bitcast.78, bf16[320,4,64]{0,2,1:T(8,128)(2,1)S(1)} %bitcast.74), kind=kOutput, calls=%fused_computation.58 | convolution fusion | flops 346030400 | bytes 12386304 | tf_op jit(solution)/shard_map/sub | solution.py:67
  35.1 5.5 fusion.7
  40.7 1.6 fusion.30
  42.3 1.2 multiply_reduce_fusion
  43.5 5.4 multiply_convert_fusion
  48.9 2.3 copy-done.1
  51.2 1.6 fusion.29
  52.9 0.1 fusion.12
  52.9 0.1 fusion.26
  53.1 3.6 collective-permute-start.2
  56.7 1.9 collective-permute-start.3
  58.6 4.3 collective-permute-done.3
  63.0 0.2 fusion.16
  63.2 1.3 convolution_convert_fusion.6
  64.6 0.0 reduce-scatter.22.cloned.1.call-start
  64.6 3.8 convolution_convert_fusion.2
  68.4 2.3 convolution_bitcast_fusion.2
  70.7 2.6 copy.27
  73.4 4.9 fusion.31
  78.4 1.3 convolution_bitcast_fusion
  79.7 2.5 copy.31
  82.3 0.0 reduce-scatter.24.cloned.1.call-start
  82.3 1.3 convolution_bitcast_fusion.1
  83.6 2.6 copy.29
  86.2 0.0 reduce-scatter.14.cloned.1.call-start
  86.2 3.2 convolution_convert_fusion.1
  89.5 3.3 convolution_convert_fusion
  92.8 2.0 reduce-scatter.18.cloned.1.call-done
  94.9 140.3 %reduce-scatter.22.cloned.1.call-done = f32[16,256]{1,0:T(8,128)} async-done(((f32[1024,256]{1,0:T(8,128)}), f32[16,256]{1,0:T(8,128)}) %reduce-scatter.22.cloned.1.call-update) | async-done | bytes 16400
  235.1 142.0 %reduce-scatter.20.cloned.1.call-done = f32[256,16]{0,1:T(8,128)} async-done(((f32[256,1024]{0,1:T(8,128)}), f32[256,16]{0,1:T(8,128)}) %reduce-scatter.20.cloned.1.call-update) | async-done | bytes 16400 | tf_op jit(solution)/shard_map/reduce_scatter | solution.py:141
  377.1 142.1 %reduce-scatter.26.cloned.1.call-done = f32[16,256]{1,0:T(8,128)} async-done(((f32[1024,256]{1,0:T(8,128)}), f32[16,256]{1,0:T(8,128)}) %reduce-scatter.26.cloned.1.call-update) | async-done | bytes 16400
  519.3 142.2 %reduce-scatter.24.cloned.1.call-done = f32[16,256]{1,0:T(8,128)} async-done(((f32[1024,256]{1,0:T(8,128)}), f32[16,256]{1,0:T(8,128)}) %reduce-scatter.24.cloned.1.call-update) | async-done | bytes 16400
  661.5 56.2 %reduce-scatter.14.cloned.1.call-done = bf16[512,1024]{1,0:T(8,128)(2,1)} async-done(((bf16[2048,1024]{1,0:T(8,128)(2,1)}), bf16[512,1024]{1,0:T(8,128)(2,1)}) %reduce-scatter.14.cloned.1.call-update) | async-done | bytes 1048592 | tf_op jit(solution)/shard_map/reduce_scatter | solution.py:75
  717.7 52.4 %reduce-scatter.16.cloned.1.call-done = bf16[512,1024]{1,0:T(8,128)(2,1)} async-done(((bf16[2048,1024]{1,0:T(8,128)(2,1)}), bf16[512,1024]{1,0:T(8,128)(2,1)}) %reduce-scatter.16.cloned.1.call-update) | async-done | bytes 1048592 | tf_op jit(solution)/shard_map/reduce_scatter | solution.py:109
  (37 shorter events, 0.4 us)
Async XLA Ops:
  7.2 11.5 %copy-start = (bf16[256,1024]{1,0:T(8,128)(2,1)S(1)}, bf16[256,1024]{1,0:T(8,128)(2,1)}, u32[]{:S(2)}) copy-start(bf16[256,1024]{1,0:T(8,128)(2,1)} %param.14) | copy-start | bytes 1572868
  7.2 87.7 %reduce-scatter.18.cloned.1.call-start = ((), (), s32[]{:S(2)}) async-start(), calls=%async_computation.9 | async-start | bytes 655360 | tf_op jit(solution)/shard_map/reduce_scatter | solution.py:119
  8.8 14.5 %copy-start.4 = (bf16[1024,256]{1,0:T(8,128)(2,1)S(1)}, bf16[1024,256]{1,0:T(8,128)(2,1)}, u32[]{:S(2)}) copy-start(bf16[1024,256]{1,0:T(8,128)(2,1)} %param.11) | copy-start | bytes 1572868
  10.5 15.1 %collective-permute-start = (bf16[32,512]{0,1:T(8,128)(2,1)S(1)}, bf16[32,512]{0,1:T(8,128)(2,1)S(1)}, u32[]{:S(2)}, u32[]{:S(2)}) collective-permute-start(bf16[32,512]{0,1:T(8,128)(2,1)S(1)} %get-tuple-element.39), channel_id=1, source_target_pairs={{0,4},{4,8},{8,12},{12,16},{16,20},{20,24},{24,28},{28,32},{32,36}... | collective-permute-start | bytes 98312 | tf_op jit(solution)/shard_map/ppermute | solution.py:15
  15.1 10.6 %collective-permute-start.1 = (bf16[32,512]{0,1:T(8,128)(2,1)S(1)}, bf16[32,512]{0,1:T(8,128)(2,1)S(1)}, u32[]{:S(2)}, u32[]{:S(2)}) collective-permute-start(bf16[32,512]{0,1:T(8,128)(2,1)S(1)} %get-tuple-element.40), channel_id=1, source_target_pairs={{4,0},{8,4},{12,8},{16,12},{20,16},{24,20},{28,24},{32,28},{36,32}... | collective-permute-start | bytes 98312 | tf_op jit(solution)/shard_map/ppermute | solution.py:18
  18.1 5.2 copy-start.8
  43.5 7.7 copy-start.3
  48.9 2.3 copy-start.1
  51.2 12.0 %copy-start.6 = (bf16[1024,256]{1,0:T(8,128)(2,1)S(1)}, bf16[1024,256]{1,0:T(8,128)(2,1)}, u32[]{:S(2)}) copy-start(bf16[1024,256]{1,0:T(8,128)(2,1)} %param.12) | copy-start | bytes 1572868
  51.2 12.0 %copy-start.7 = (bf16[1024,256]{1,0:T(8,128)(2,1)S(1)}, bf16[1024,256]{1,0:T(8,128)(2,1)}, u32[]{:S(2)}) copy-start(bf16[1024,256]{1,0:T(8,128)(2,1)} %param.13) | copy-start | bytes 1572868
  53.1 5.6 collective-permute-start.2
  56.7 6.3 collective-permute-start.3
  64.6 170.6 %reduce-scatter.22.cloned.1.call-start = ((), (), s32[]{:S(2)}) async-start(), calls=%async_computation.11 | async-start | bytes 1064960
  64.6 3.8 copy-start.9
  73.3 5.1 copy-start.2
  73.3 303.8 %reduce-scatter.20.cloned.1.call-start = ((), (), s32[]{:S(2)}) async-start(), calls=%async_computation.10 | async-start | bytes 1064960 | tf_op jit(solution)/shard_map/reduce_scatter | solution.py:141
  78.4 440.9 %reduce-scatter.26.cloned.1.call-start = ((), (), s32[]{:S(2)}) async-start(), calls=%async_computation.13 | async-start | bytes 1064960
  82.3 579.2 %reduce-scatter.24.cloned.1.call-start = ((), (), s32[]{:S(2)}) async-start(), calls=%async_computation.12 | async-start | bytes 1064960
  86.2 3.4 copy-start.5
  86.2 631.5 %reduce-scatter.14.cloned.1.call-start = ((), (), s32[]{:S(2)}) async-start(), calls=%async_computation.7 | async-start | bytes 5242880 | tf_op jit(solution)/shard_map/reduce_scatter | solution.py:75
  89.5 680.6 %reduce-scatter.16.cloned.1.call-start = ((), (), s32[]{:S(2)}) async-start(), calls=%async_computation.8 | async-start | bytes 5242880 | tf_op jit(solution)/shard_map/reduce_scatter | solution.py:109
Sparse Core Ops, SparseCore 0:
  64.7 30.1 reduce-scatter.17
  99.4 135.6 reduce-scatter.21
  239.7 137.3 reduce-scatter.19
  381.5 137.6 reduce-scatter.25
  523.7 137.7 reduce-scatter.23
  664.4 53.1 reduce-scatter.13
  720.9 49.1 reduce-scatter.15
where the time goes:
time: 777 us
  waiting for transfers between devices  682 us (88%)
  matrix products  49.6 us (6%)
  between operations  14.4 us (2%)
  starting transfers between devices  12.3 us (2%)
  local copies, waits for them, and re-layouts  10.4 us (1%)
  other arithmetic  8.47 us (1%)
    unnamed x10, waiting for transfers between devices  425 us
    reduce_scatter x1, waiting for transfers between devices, on_device(): lax.psum_scatter(out_term_w, 'seq', scatter_dimension=1, tiled=True)  142 us
    reduce_scatter x1, waiting for transfers between devices, on_device(): lax.psum_scatter(jnp.dot(part_rows, w_out, preferred_element_type=jnp.flo...  56.2 us
    reduce_scatter x1, waiting for transfers between devices, on_device(): lax.psum_scatter(lax.dot_general(part_rows, w_query, (((1,), (1,)), ((),...  52.4 us
  transfers between devices with their start and end apart: 11, of which 8 were waited for; matrix products, arithmetic and copies ran while one was open for 5% of the time, Pallas kernels for 0%

commit v1 on v0

v1 whole, which is shorter than its diff:
```python
import jax
import jax.numpy as jnp
from jax import lax
from jax.experimental import pallas as pl
from jax.experimental.pallas import tpu as pltpu
from jax.sharding import PartitionSpec as P

HEAD_DIM = 64
WINDOW = 32
HEADS = 4
COLS = HEADS * HEAD_DIM
D = 1024
F_DEV = 2048
S_DEV = 256
EXT = S_DEV + 2 * WINDOW
TILE = 512
SUB = 256
NARROW = 160
RANGES = 64
LOG2E = 1.4426950408889634
MESH = pl.DeviceIdType.MESH
BF = jnp.bfloat16
F32 = jnp.float32
NN = (((1,), (0,)), ((), ()))
NT = (((1,), (1,)), ((), ()))
TN = (((0,), (0,)), ((), ()))


def mm(left, right, dims):
    return lax.dot_general(left, right, dims, preferred_element_type=F32)


def attention_kernel(starts_ref, narrow_ref, frames_ref, cot_ref, text_ref, low_ref, high_ref,
                     wqt_ref, wk_ref, wv_ref, wo_ref, bounds_ref,
                     att_ref, dq_ref, gk_ref, gv_ref,
                     k_s, v_s, qt_s, ut_s):
    step = pl.program_id(0)

    @pl.when(step == 0)
    def _():
        text = jnp.concatenate([low_ref[...], text_ref[...], high_ref[...]], axis=0)
        keys = mm(text, wk_ref[...], NN).astype(BF)
        vals = mm(text, wv_ref[...], NN).astype(BF)
        for h in range(HEADS):
            k_s[h] = keys[:, h * HEAD_DIM:(h + 1) * HEAD_DIM]
            v_s[h] = vals[:, h * HEAD_DIM:(h + 1) * HEAD_DIM]
        gk_ref[...] = jnp.zeros_like(gk_ref)
        gv_ref[...] = jnp.zeros_like(gv_ref)

    qt_s[...] = mm(wqt_ref[...], frames_ref[...], NT).astype(BF)
    ut_s[...] = mm(wo_ref[...], cot_ref[...], NT).astype(BF)

    def process(sub, start, rows):
        lanes = pl.ds(sub * SUB, SUB)
        here = pl.ds(start, rows)
        low = bounds_ref[0:1, lanes]
        high = bounds_ref[1:2, lanes]
        state = lax.broadcasted_iota(jnp.int32, (rows, SUB), 0) + start
        allowed = (state >= low) & (state <= high)
        for h in range(HEADS):
            cols = pl.ds(h * HEAD_DIM, HEAD_DIM)
            q = qt_s[cols, lanes]
            u = ut_s[cols, lanes]
            k = k_s[h, here, :]
            v = v_s[h, here, :]
            s = jnp.where(allowed, mm(k, q, NN), -jnp.inf)
            top = jnp.max(s, axis=0, keepdims=True)
            e = jnp.exp2((s - top) * (LOG2E * HEAD_DIM ** -0.5))
            p = e * (1.0 / jnp.sum(e, axis=0, keepdims=True))
            pb = p.astype(BF)
            att = mm(v, pb, TN).astype(BF)
            att_ref[cols, lanes] = att
            delta = jnp.sum(u.astype(F32) * att.astype(F32), axis=0, keepdims=True)
            ds = (p * (mm(v, u, NN) - delta) * HEAD_DIM ** -0.5).astype(BF)
            dq_ref[cols, lanes] = mm(k, ds, TN).astype(BF)
            gk_ref[h, here, :] += mm(ds, q, NT)
            gv_ref[h, here, :] += mm(pb, u, NT)

    @pl.loop(0, TILE // SUB)
    def _(sub):
        index = step * (TILE // SUB) + sub
        start = pl.multiple_of(starts_ref[index], 16)

        @pl.when(narrow_ref[index] == 1)
        def _():
            process(sub, start, NARROW)

        @pl.when(narrow_ref[index] == 0)
        def _():
            process(sub, 0, EXT)


def attention(frames, cot, text, low, high, wqt, wk, wv, wo, bounds, starts, narrow):
    whole = lambda *shape: pl.BlockSpec(shape, lambda i, *_: (0,) * len(shape))
    return pl.pallas_call(
        attention_kernel,
        grid_spec=pltpu.PrefetchScalarGridSpec(
            num_scalar_prefetch=2,
            grid=(F_DEV // TILE,),
            in_specs=[
                pl.BlockSpec((TILE, D), lambda i, *_: (i, 0)),
                pl.BlockSpec((TILE, D), lambda i, *_: (i, 0)),
                whole(S_DEV, D), whole(WINDOW, D), whole(WINDOW, D),
                whole(COLS, D), whole(D, COLS), whole(D, COLS), whole(COLS, D),
                pl.BlockSpec((2, TILE), lambda i, *_: (0, i)),
            ],
            out_specs=[
                pl.BlockSpec((COLS, TILE), lambda i, *_: (0, i)),
                pl.BlockSpec((COLS, TILE), lambda i, *_: (0, i)),
                whole(HEADS, EXT, HEAD_DIM), whole(HEADS, EXT, HEAD_DIM),
            ],
            scratch_shapes=[
                pltpu.VMEM((HEADS, EXT, HEAD_DIM), BF),
                pltpu.VMEM((HEADS, EXT, HEAD_DIM), BF),
                pltpu.VMEM((COLS, TILE), BF),
                pltpu.VMEM((COLS, TILE), BF),
            ],
        ),
        out_shape=[
            jax.ShapeDtypeStruct((COLS, F_DEV), BF),
            jax.ShapeDtypeStruct((COLS, F_DEV), BF),
            jax.ShapeDtypeStruct((HEADS, EXT, HEAD_DIM), F32),
            jax.ShapeDtypeStruct((HEADS, EXT, HEAD_DIM), F32),
        ],
        compiler_params=pltpu.CompilerParams(vmem_limit_bytes=40 * 2 ** 20),
        cost_estimate=pl.CostEstimate(flops=8 * 10 ** 9, bytes_accessed=14 * 10 ** 6, transcendentals=3 * 10 ** 6),
    )(starts, narrow, frames, cot, text, low, high, wqt, wk, wv, wo, bounds)


def reduce_kernel(att_ref, dq_ref, inner_ref, edges_ref, text_ref, wk_ref, wv_ref, wall_ref, frames_hbm, cot_hbm,
                  layer_ref, fgrad_ref, tgrad_ref, wgrad_ref,
                  frames_s, cot_s, far_att, far_dq, far_edge, kv_s, term_s, near_s, sum_c, far_x, sum_x, far_z,
                  tterm_s, far_t, load_sem,
                  send_a, recv_a, send_e, recv_e, send_c, recv_c, send_x, recv_x, send_z, recv_z, send_t, recv_t):
    seq, head = lax.axis_index("seq"), lax.axis_index("head")
    core, x, z = seq % 2, (seq // 2) % 4, seq // 8
    rows_of = lambda d: (head + d) % 4
    x_of = lambda d: (x + d) % 4
    z_of = lambda d: (z + d) % 8
    at_y = lambda d: (seq, rows_of(d))
    at_x = lambda d: (z * 8 + x_of(d) * 2 + core, head)
    at_z = lambda d: (z_of(d) * 8 + x * 2 + core, head)
    at_core = (z * 8 + x * 2 + (1 - core), head)
    at_next = ((seq + 1) % RANGES, head)
    at_prev = ((seq + RANGES - 1) % RANGES, head)

    load_cot = pltpu.make_async_copy(cot_hbm, cot_s, load_sem.at[0])
    load_cot.start()
    load_frames = pltpu.make_async_copy(frames_hbm, frames_s, load_sem.at[1])
    load_frames.start()

    peers = [at_y(d) for d in (1, 2, 3)] + [at_x(d) for d in (1, 2, 3)] + [at_z(d) for d in range(1, 8)]
    peers += [at_core, at_next, at_prev]
    barrier = pltpu.get_barrier_semaphore()
    for peer in peers:
        pl.semaphore_signal(barrier, inc=1, device_id=peer, device_id_type=MESH)
    pl.semaphore_wait(barrier, len(peers))

    def send(src, dst, sends, recvs, index, peer):
        copy = pltpu.make_async_remote_copy(src_ref=src, dst_ref=dst, send_sem=sends.at[index], recv_sem=recvs.at[index],
                                            device_id=peer, device_id_type=MESH)
        copy.start()
        return copy

    edge_copies = [send(edges_ref.at[0], far_edge.at[0], send_e, recv_e, 0, at_prev),
                   send(edges_ref.at[1], far_edge.at[1], send_e, recv_e, 1, at_next)]
    att_copies, dq_copies = {}, {}
    for d in (2, 1, 3):
        lanes = pl.ds(pl.multiple_of(rows_of(d) * TILE, TILE), TILE)
        att_copies[d] = send(att_ref.at[:, lanes], far_att.at[d - 1], send_a, recv_a, d - 1, at_y(d))
    for d in (2, 1, 3):
        lanes = pl.ds(pl.multiple_of(rows_of(d) * TILE, TILE), TILE)
        dq_copies[d] = send(dq_ref.at[:, lanes], far_dq.at[d - 1], send_a, recv_a, d + 2, at_y(d))

    def put(group, width_at, value, block):
        for part in range(2):
            for chip in range(4):
                for side in range(2):
                    at = part * 128 + chip * 32 + side * 16
                    term_s[group, side, chip, block * 2 + part, :, :] = value[at:at + 16]

    def frame_term(group, left_ref, right_s):
        @pl.loop(0, 4)
        def _(block):
            lanes = pl.ds(pl.multiple_of(block * 256, 256), 256)
            value = mm(left_ref[...], right_s[:, lanes], NN)
            put(group, 0, jnp.transpose(value).astype(BF), block)

    def core_send(group):
        return send(term_s.at[group, 1 - core], near_s.at[group], send_c, recv_c, group, at_core)

    load_cot.wait()
    frame_term(0, att_ref, cot_s)
    core_copies = [core_send(0)]
    load_frames.wait()
    frame_term(1, dq_ref, frames_s)
    core_copies.append(core_send(1))
    for copy in edge_copies:
        copy.wait()
    kv_s[...] = inner_ref[...].astype(BF)
    kv_s[:WINDOW] = (inner_ref[:WINDOW] + far_edge[1].astype(F32)).astype(BF)
    kv_s[S_DEV - WINDOW:] = (inner_ref[S_DEV - WINDOW:] + far_edge[0].astype(F32)).astype(BF)

    for which in range(2):
        @pl.loop(0, 4)
        def _(block):
            lanes = pl.ds(pl.multiple_of(block * 256, 256), 256)
            value = mm(text_ref[:, lanes], kv_s[:, which * COLS:(which + 1) * COLS], TN)
            put(2 + which, 0, value.astype(BF), block)
        core_copies.append(core_send(2 + which))

    for part in range(4):
        rows = slice(part * 64, part * 64 + 64)
        value = mm(kv_s[rows, :COLS], wk_ref[...], NT) + mm(kv_s[rows, COLS:], wv_ref[...], NT)
        tterm_s[part] = value.astype(BF)
    text_copies = [send(tterm_s.at[rows_of(d)], far_t.at[d - 1], send_t, recv_t, d - 1, at_y(d)) for d in (2, 1, 3)]

    x_copies = []
    for group in range(4):
        core_copies[group].wait()

        @pl.loop(0, 4)
        def _(chip):
            sum_c[group, chip] = (term_s[group, core, chip].astype(F32) + near_s[group, chip].astype(F32)).astype(BF)
        x_copies.append([send(sum_c.at[group, x_of(d)], far_x.at[group, d - 1], send_x, recv_x, group * 3 + d - 1, at_x(d))
                         for d in (2, 1, 3)])

    z_copies = []
    for group in range(4):
        for copy in x_copies[group]:
            copy.wait()
        total = sum_c[group, x].astype(F32)
        for d in range(3):
            total = total + far_x[group, d].astype(F32)
        sum_x[group] = total.astype(BF)
        z_copies.append([send(sum_x.at[group, z_of(d)], far_z.at[group, d - 1], send_z, recv_z, group * 7 + d - 1, at_z(d))
                         for d in (4, 3, 5, 2, 6, 1, 7)])

    def project(mine_ref, far, first, out_ref):
        mine = pl.ds(pl.multiple_of(head * TILE, TILE), TILE)
        parts = [jnp.transpose(mine_ref[:, mine])] + [jnp.transpose(far[d - 1]) for d in (1, 2, 3)]
        origin = [head] + [(head + 4 - d) % 4 for d in (1, 2, 3)]
        for block in range(4):
            lanes = slice(block * 256, block * 256 + 256)
            total = None
            for part, source in zip(parts, origin):
                term = mm(part, wall_ref[source, first:first + COLS, lanes], NN).astype(BF).astype(F32)
                total = term if total is None else total + term
            out_ref[:, lanes] = total.astype(BF)

    for copy in att_copies.values():
        copy.wait()
    project(att_ref, far_att, 0, layer_ref)
    for copy in dq_copies.values():
        copy.wait()
    project(dq_ref, far_dq, COLS, fgrad_ref)

    for copy in text_copies:
        copy.wait()
    total = tterm_s[head].astype(F32)
    for d in range(3):
        total = total + far_t[d].astype(F32)
    tgrad_ref[...] = total.astype(BF)

    for group in range(4):
        for copy in z_copies[group]:
            copy.wait()
        total = sum_x[group, z].astype(F32)
        for d in range(7):
            total = total + far_z[group, d].astype(F32)
        wgrad_ref[group] = total


def reduce_all(att, dq, inner, edges, text, wk, wv, wall, frames, cot):
    vmem = pl.BlockSpec(memory_space=pltpu.VMEM)
    hbm = pl.BlockSpec(memory_space=pl.ANY)
    dma = pltpu.SemaphoreType.DMA
    return pl.pallas_call(
        reduce_kernel,
        in_specs=[vmem] * 8 + [hbm] * 2,
        out_specs=[vmem] * 4,
        out_shape=[
            jax.ShapeDtypeStruct((TILE, D), BF),
            jax.ShapeDtypeStruct((TILE, D), BF),
            jax.ShapeDtypeStruct((64, D), BF),
            jax.ShapeDtypeStruct((4, 16, COLS), F32),
        ],
        scratch_shapes=[
            pltpu.VMEM((F_DEV, D), BF),
            pltpu.VMEM((F_DEV, D), BF),
            pltpu.VMEM((3, COLS, TILE), BF),
            pltpu.VMEM((3, COLS, TILE), BF),
            pltpu.VMEM((2, WINDOW, 2 * COLS), BF),
            pltpu.VMEM((S_DEV, 2 * COLS), BF),
            pltpu.VMEM((4, 2, 4, 8, 16, COLS), BF),
            pltpu.VMEM((4, 4, 8, 16, COLS), BF),
            pltpu.VMEM((4, 4, 8, 16, COLS), BF),
            pltpu.VMEM((4, 3, 8, 16, COLS), BF),
            pltpu.VMEM((4, 8, 16, COLS), BF),
            pltpu.VMEM((4, 7, 16, COLS), BF),
            pltpu.VMEM((4, 64, D), BF),
            pltpu.VMEM((3, 64, D), BF),
            dma((2,)),
            dma((6,)), dma((6,)), dma((2,)), dma((2,)), dma((4,)), dma((4,)), dma((12,)), dma((12,)),
            dma((28,)), dma((28,)), dma((3,)), dma((3,)),
        ],
        compiler_params=pltpu.CompilerParams(collective_id=0, has_side_effects=True, vmem_limit_bytes=56 * 2 ** 20),
        cost_estimate=pl.CostEstimate(flops=7 * 10 ** 9, bytes_accessed=20 * 10 ** 6, transcendentals=0),
    )(att, dq, inner, edges, text, wk, wv, wall, frames, cot)


def on_device(frames, text_states, durations, w_query, w_key, w_value, w_out, cotangent):
    shard = lax.axis_index("seq")
    wqt = jnp.transpose(w_query)
    wall = lax.all_gather(jnp.concatenate([w_out, wqt], axis=0), "head", axis=0)
    low = lax.ppermute(text_states[S_DEV - WINDOW:], "seq", [(i, (i + 1) % RANGES) for i in range(RANGES)])
    high = lax.ppermute(text_states[:WINDOW], "seq", [(i, (i - 1) % RANGES) for i in range(RANGES)])

    ends = jnp.cumsum(durations[0], dtype=jnp.int32)
    own = jnp.sum((ends[:, None] <= jnp.arange(F_DEV, dtype=jnp.int32)[None, :]).astype(jnp.int32), axis=0, dtype=jnp.int32)
    first = jnp.where(shard == 0, WINDOW, 0)
    last = EXT - 1 - jnp.where(shard == RANGES - 1, WINDOW, 0)
    bounds = jnp.stack([jnp.maximum(own, first), jnp.minimum(own + 2 * WINDOW, last)])
    starts = jnp.minimum((own[::SUB] // 16) * 16, EXT - NARROW)
    narrow = (own[SUB - 1::SUB] + 2 * WINDOW < starts + NARROW).astype(jnp.int32)

    att, dq, gk, gv = attention(frames, cotangent, text_states, low, high, wqt, w_key, w_value, w_out, bounds, starts, narrow)
    both = jnp.concatenate([jnp.transpose(gk, (1, 0, 2)).reshape(EXT, COLS), jnp.transpose(gv, (1, 0, 2)).reshape(EXT, COLS)], axis=1)
    inner = both[WINDOW:WINDOW + S_DEV]
    edges = jnp.stack([both[:WINDOW], both[WINDOW + S_DEV:]]).astype(BF)
    layer, fgrad, tgrad, wgrad = reduce_all(att, dq, inner, edges, text_states, w_key, w_value, wall, frames, cotangent)
    return layer, fgrad, tgrad, wgrad[1], wgrad[2], wgrad[3], jnp.transpose(wgrad[0])


def solution(mesh):
    placed = (
        P("seq", None),
        P("seq", None),
        P("seq", None),
        P(None, "head"),
        P(None, "head"),
        P(None, "head"),
        P("head", None),
        P("seq", None),
    )
    return jax.shard_map(
        on_device,
        mesh=mesh,
        in_specs=placed,
        out_specs=(
            P(("seq", "head"), None),
            P(("seq", "head"), None),
            P(("seq", "head"), None),
            P("seq", "head"),
            P("seq", "head"),
            P("seq", "head"),
            P("head", "seq"),
        ),
        check_vma=False,
    )
```

time: 777 us -> 119 us (0.15)
  waiting for transfers between devices: 682 us -> 19.5 us
  Pallas kernels: 0 us -> 61.4 us
  matrix products: 49.6 us -> 0 us
  starting transfers between devices: 12.3 us -> 3.36 us
    unnamed x10 -> x1, waiting for transfers between devices: 425 us -> 0.02 us
    reduce_scatter x4 -> x0, waiting for transfers between devices: 253 us -> none  [the longest x1 142 us: on_device(): lax.psum_scatter(out_term_w, 'seq', scatter_dimension=1, tiled=True)]
    pallas_call x0 -> x2, Pallas kernels: none -> 61.4 us  [the longest x1 40.5 us: reduce_all(): pl.pallas_call(reduce_kernel, in_specs=[vmem] * 8 + [hbm] * 2, out_specs=...]
    dot_general x16 -> x0, matrix products: 40.4 us -> none  [the longest x1 5.37 us: on_device(): jnp.einsum('fhd,khd->hfk', up_heads, val_heads, preferred_element_type=jn...]
    all_gather x0 -> x1, waiting for transfers between devices: none -> 14.2 us  [on_device(): wall = lax.all_gather(jnp.concatenate([w_out, wqt], axis=0), 'head', axis=0)]
    sub x1 -> x0, matrix products: 9.23 us -> none  [on_device(): shifted = jnp.exp(scores - largest)]
    ppermute x4 -> x2, starting transfers between devices: 12 us -> 3.32 us  [the longest x1 3.32 us: on_device(): lax.ppermute(text_states[:WINDOW], 'seq', [(i, (i - 1) % RANGES) for i in...]
  transfers between devices with their start and end apart: 11 -> 3, of which waited for: 8 -> 3; matrix products, arithmetic and copies ran while one was open for 5% -> 3% of each run, Pallas kernels for 0% -> 18%
where the time goes in v1:
time: 119 us; the launch traced here: 118 us
  Pallas kernels  61.4 us (52%)
  waiting for transfers between devices  19.5 us (16%)
  local copies, waits for them, and re-layouts  15.3 us (13%)
  between operations  14.2 us (12%)
  other arithmetic  4.43 us (4%)
  starting transfers between devices  3.36 us (3%)
    pallas_call x1, Pallas kernels, reduce_all(): pl.pallas_call(reduce_kernel, in_specs=[vmem] * 8 + [hbm] * 2, out_specs=...  40.5 us
    pallas_call x1, Pallas kernels, attention(): pl.pallas_call(attention_kernel, grid_spec=pltpu.PrefetchScalarGridSpec(n...  21 us
    all_gather x1, waiting for transfers between devices, on_device(): wall = lax.all_gather(jnp.concatenate([w_out, wqt], axis=0), 'head', axis=0)  14.2 us
    unnamed x26, local copies, waits for them, and re-layouts  12.7 us
    ppermute x1, waiting for transfers between devices, on_device(): lax.ppermute(text_states[S_DEV - WINDOW:], 'seq', [(i, (i + 1) % RANGES)...  5.19 us
    ppermute x1, starting transfers between devices, on_device(): lax.ppermute(text_states[:WINDOW], 'seq', [(i, (i - 1) % RANGES) for i in...  3.32 us
  transfers between devices with their start and end apart: 3, of which 3 were waited for; matrix products, arithmetic and copies ran while one was open for 3% of the time, Pallas kernels for 18%

profile of v1, /device:TPU:1, one launch (start us, length us, event | category | flops | bytes accessed | tf_op | source)
XLA Modules:
  0.0 118.3 jit_solution(14869836069705904461)
XLA Ops:
  7.2 0.0 copy-start
  7.2 0.0 copy-start.1
  7.2 0.0 copy-start.10
  7.2 0.0 copy-start.4
  7.2 0.0 all-gather.3.cloned.1.call-start
  7.3 1.3 %copy.23 = bf16[1024,256]{0,1:T(8,128)(2,1)S(1)} copy(bf16[1024,256]{1,0:T(8,128)(2,1)} %param.11) | data formatting | bytes 1048576 | tf_op args[3]
  8.6 2.1 %pad_maximum_fusion = bf16[512,1024]{1,0:T(8,128)(2,1)} fusion(bf16[256,1024]{1,0:T(8,128)(2,1)S(1)} %bitcast.25, bf16[256,1024]{1,0:T(8,128)(2,1)} %wo_ref.1), kind=kLoop, calls=%fused_computation.2 | loop fusion | flops 2097152 | bytes 2097152 | tf_op jit(solution)/shard_map/concatenate | solution.py:315
  10.7 0.0 all-gather.3.cloned.1.call-update
  10.7 0.0 copy-done.1
  10.7 3.3 %collective-permute-start.1 = (bf16[32,1024]{1,0:T(8,128)(2,1)S(1)}, bf16[32,1024]{1,0:T(8,128)(2,1)S(1)}, u32[]{:S(2)}, u32[]{:S(2)}) collective-permute-start(bf16[32,1024]{1,0:T(8,128)(2,1)S(1)} %get-tuple-element.25), channel_id=1, source_target_pairs={{0,252},{4,0},{8,4},{12,8},{16,12},{20,16},{24,20},{28,24},{32,28}... | collective-permute-start | bytes 196616 | tf_op jit(solution)/shard_map/ppermute | solution.py:317
  14.1 0.0 collective-permute-start
  14.1 0.0 copy-done.10
  14.1 0.3 reduce-window.9
  14.4 0.1 slice.42
  14.5 0.1 slice_reduce_fusion
  14.6 0.1 add_bitcast_fusion
  14.7 0.3 convert_reduce_fusion
  15.0 0.1 slice.45
  15.1 0.1 slice.44
  15.3 0.1 collective-permute-done.1.high_ref
  15.4 5.2 %collective-permute-done.low_ref = bf16[32,1024]{1,0:T(8,128)(2,1)S(1)} collective-permute-done((bf16[32,1024]{1,0:T(8,128)(2,1)S(1)}, bf16[32,1024]{1,0:T(8,128)(2,1)S(1)}, u32[]{:S(2)}, u32[]{:S(2)}) %collective-permute-start) | collective-permute-done | bytes 65568 | tf_op jit(solution)/shard_map/ppermute | solution.py:316
  20.6 0.0 copy-done
  20.6 0.0 copy-done.4
  20.6 0.0 copy-start.2
  20.6 2.2 %copy-done.2 = bf16[2048,1024]{1,0:T(8,128)(2,1)S(1)} copy-done((bf16[2048,1024]{1,0:T(8,128)(2,1)S(1)}, bf16[2048,1024]{1,0:T(8,128)(2,1)}, u32[]{:S(2)}) %copy-start.2) | copy-done | bytes 4194328
  22.8 0.0 copy-start.3
  22.8 2.2 %copy-done.3 = bf16[2048,1024]{1,0:T(8,128)(2,1)S(1)} copy-done((bf16[2048,1024]{1,0:T(8,128)(2,1)S(1)}, bf16[2048,1024]{1,0:T(8,128)(2,1)}, u32[]{:S(2)}) %copy-start.3) | copy-done | bytes 4194328
  25.0 0.0 copy-start.5
  25.0 1.1 copy-done.5
  26.0 21.0 %shard_map.135 = (bf16[256,2048]{1,0:T(8,128)(2,1)S(1)}, bf16[256,2048]{1,0:T(8,128)(2,1)S(1)}, f32[4,320,64]{2,1,0:T(8,128)S(1)}, f32[4,320,64]{2,1,0:T(8,128)S(1)}) custom-call(s32[8]{0:T(128)S(1)} %get-tuple-element.24.starts_ref, s32[8]{0:T(128)S(1)} %get-tuple-element.23.narrow_ref, bf16[2048,1024]{1,0:T(8,128)(2,1)S(1)} %copy-done.2, ...), custom_call_target="tpu_custom_call" | custom-call | flops 8000000000 | bytes 14000000 | tf_op jit(solution)/shard_map/pallas_call | solution.py:95
  47.0 0.0 copy-start.6
  47.0 1.0 copy-done.6
  48.0 1.0 copy-done.7
  49.0 0.2 copy.24
  49.2 0.1 copy.26
  49.4 0.2 copy.25
  49.6 0.1 copy.27
  49.8 0.6 pad_maximum_fusion.2.edges_ref
  50.5 0.9 fusion.1.inner_ref
  51.3 14.2 %all-gather.3.cloned.1.call-done = bf16[2048,1024]{1,0:T(8,128)(2,1)} async-done(((bf16[512,1024]{1,0:T(8,128)(2,1)}), bf16[2048,1024]{1,0:T(8,128)(2,1)}) %all-gather.3.cloned.1.call-update) | async-done | bytes 4194320 | tf_op jit(solution)/shard_map/all_gather | solution.py:315
  65.5 40.5 %shard_map.136 = (bf16[512,1024]{1,0:T(8,128)(2,1)}, bf16[512,1024]{1,0:T(8,128)(2,1)}, bf16[64,1024]{1,0:T(8,128)(2,1)}, f32[4,16,256]{2,1,0:T(8,128)}) custom-call(bf16[256,2048]{1,0:T(8,128)(2,1)} %copy-done.6, bf16[256,2048]{1,0:T(8,128)(2,1)} %copy-done.7, f32[256,512]{1,0:T(8,128)} %fusion.1.inner_ref, ...), custom_call_target="tpu_custom_call" | custom-call | flops 7000000000 | bytes 20000000 | tf_op jit(solution)/shard_map/pallas_call | solution.py:278
  106.0 0.0 copy-start.8
  106.0 1.5 %slice_bitcast_fusion.2 = (f32[256,16]{0,1:T(8,128)}, f32[16,256]{1,0:T(8,128)}, f32[16,256]{1,0:T(8,128)}, f32[16,256]{1,0:T(8,128)}) fusion(f32[4,16,256]{2,1,0:T(8,128)} %get-tuple-element.22), kind=kLoop, calls=%fused_computation.12 | loop fusion | bytes 131072 | tf_op jit(solution)/shard_map/transpose | solution.py:332
  107.5 2.3 %copy.31 = bf16[512,1024]{1,0:T(8,128)(2,1)} copy(bf16[512,1024]{1,0:T(8,128)(2,1)} %get-tuple-element.42) | data formatting | bytes 2097152
  109.8 0.0 copy-done.8
  109.8 1.0 copy.32
  110.8 0.0 copy-done.9
  110.8 0.7 copy.33
  (9 shorter events, 0.1 us)
Async XLA Ops:
  7.2 13.4 %copy-start = (bf16[256,1024]{1,0:T(8,128)(2,1)S(1)}, bf16[256,1024]{1,0:T(8,128)(2,1)}, u32[]{:S(2)}) copy-start(bf16[256,1024]{1,0:T(8,128)(2,1)} %wo_ref.1) | copy-start | bytes 1572868
  7.2 3.5 %copy-start.1 = (bf16[256,1024]{1,0:T(8,128)(2,1)S(1)}, bf16[256,1024]{1,0:T(8,128)(2,1)}, u32[]{:S(2)}) copy-start(bf16[256,1024]{1,0:T(8,128)(2,1)} %text_ref.3) | copy-start | bytes 1572868
  7.2 6.9 %copy-start.10 = (s32[1,256]{1,0:T(1,128)S(1)}, s32[1,256]{1,0:T(1,128)}, u32[]{:S(2)}) copy-start(s32[1,256]{1,0:T(1,128)} %param.10) | copy-start | bytes 3076
  7.2 13.4 %copy-start.4 = (bf16[1024,256]{1,0:T(8,128)(2,1)S(1)}, bf16[1024,256]{1,0:T(8,128)(2,1)}, u32[]{:S(2)}) copy-start(bf16[1024,256]{1,0:T(8,128)(2,1)} %wk_ref.3) | copy-start | bytes 1572868
  7.2 58.3 %all-gather.3.cloned.1.call-start = ((), (), s32[]{:S(2)}) async-start(), calls=%async_computation | async-start | bytes 5242880 | tf_op jit(solution)/shard_map/all_gather | solution.py:315
  10.7 4.6 %collective-permute-start.1 = (bf16[32,1024]{1,0:T(8,128)(2,1)S(1)}, bf16[32,1024]{1,0:T(8,128)(2,1)S(1)}, u32[]{:S(2)}, u32[]{:S(2)}) collective-permute-start(bf16[32,1024]{1,0:T(8,128)(2,1)S(1)} %get-tuple-element.25), channel_id=1, source_target_pairs={{0,252},{4,0},{8,4},{12,8},{16,12},{20,16},{24,20},{28,24},{32,28}... | collective-permute-start | bytes 196616 | tf_op jit(solution)/shard_map/ppermute | solution.py:317
  14.1 6.5 %collective-permute-start = (bf16[32,1024]{1,0:T(8,128)(2,1)S(1)}, bf16[32,1024]{1,0:T(8,128)(2,1)S(1)}, u32[]{:S(2)}, u32[]{:S(2)}) collective-permute-start(bf16[32,1024]{1,0:T(8,128)(2,1)S(1)} %get-tuple-element.26), channel_id=1, source_target_pairs={{0,4},{4,8},{8,12},{12,16},{16,20},{20,24},{24,28},{28,32},{32,36}... | collective-permute-start | bytes 196616 | tf_op jit(solution)/shard_map/ppermute | solution.py:316
  20.6 2.2 %copy-start.2 = (bf16[2048,1024]{1,0:T(8,128)(2,1)S(1)}, bf16[2048,1024]{1,0:T(8,128)(2,1)}, u32[]{:S(2)}) copy-start(bf16[2048,1024]{1,0:T(8,128)(2,1)} %frames_hbm.1) | copy-start | bytes 12582916
  22.8 2.2 %copy-start.3 = (bf16[2048,1024]{1,0:T(8,128)(2,1)S(1)}, bf16[2048,1024]{1,0:T(8,128)(2,1)}, u32[]{:S(2)}) copy-start(bf16[2048,1024]{1,0:T(8,128)(2,1)} %cot_hbm.1) | copy-start | bytes 12582916
  25.0 1.1 copy-start.5
  47.0 1.0 copy-start.6
  48.0 1.0 copy-start.7
  106.0 3.8 %copy-start.8 = (bf16[512,1024]{1,0:T(8,128)(2,1)S(1)}, bf16[512,1024]{1,0:T(8,128)(2,1)}, u32[]{:S(2)}) copy-start(bf16[512,1024]{1,0:T(8,128)(2,1)} %get-tuple-element.43) | copy-start | bytes 3145732
  107.5 3.3 %copy-start.9 = (bf16[64,1024]{1,0:T(8,128)(2,1)S(1)}, bf16[64,1024]{1,0:T(8,128)(2,1)}, u32[]{:S(2)}) copy-start(bf16[64,1024]{1,0:T(8,128)(2,1)} %get-tuple-element.44) | copy-start | bytes 393220
Sparse Core Ops, SparseCore 0:
  10.8 54.6 all-gather.2

commit v2 on v1

v2 whole, which is shorter than its diff:
```python
import jax
import jax.numpy as jnp
from jax import lax
from jax.experimental import pallas as pl
from jax.experimental.pallas import tpu as pltpu
from jax.sharding import PartitionSpec as P

HEAD_DIM = 64
WINDOW = 32
HEADS = 4
COLS = HEADS * HEAD_DIM
D = 1024
F_DEV = 2048
S_DEV = 256
EXT = S_DEV + 2 * WINDOW
TILE = 512
SUB = 256
SPAN = 272
RANGES = 64
LOG2E = 1.4426950408889634
MESH = pl.DeviceIdType.MESH
BF = jnp.bfloat16
F32 = jnp.float32
NN = (((1,), (0,)), ((), ()))
NT = (((1,), (1,)), ((), ()))
TN = (((0,), (0,)), ((), ()))


def mm(left, right, dims):
    return lax.dot_general(left, right, dims, preferred_element_type=F32)


def kernel(frames_hbm, cot_hbm, text_hbm, dur_ref, wq_hbm, wk_hbm, wv_hbm, wo_hbm,
           layer_ref, fgrad_ref, tgrad_ref, wgrad_ref,
           frames_s, cot_s, text_s, wq_s, wk_s, wv_s, wcat_s, wall_s,
           k_s, v_s, qt_s, ut_s, gk_s, gv_s, ends_s, att_s, dq_s,
           far_att, far_dq, edge_s, far_edge, kv_s, term_s, near_s, sum_c, far_x, sum_x, far_z, tterm_s, far_t,
           load_w, load_f, load_c,
           send_h, recv_h, send_wy, recv_wy, send_wx, recv_wx, send_wc, recv_wc,
           send_a, recv_a, send_b, recv_b, send_e, recv_e, send_c, recv_c, send_x, recv_x, send_z, recv_z, send_t, recv_t):
    seq, head = lax.axis_index("seq"), lax.axis_index("head")
    core, x, z = seq % 2, (seq // 2) % 4, seq // 8
    y_of = lambda d: (head + d) % 4
    x_of = lambda d: (x + d) % 4
    z_of = lambda d: (z + d) % 8
    at_y = lambda d: (seq, y_of(d))
    at_x = lambda d: (z * 8 + x_of(d) * 2 + core, head)
    at_z = lambda d: (z_of(d) * 8 + x * 2 + core, head)
    at_core = (z * 8 + x * 2 + (1 - core), head)
    at_next = ((seq + 1) % RANGES, head)
    at_prev = ((seq + RANGES - 1) % RANGES, head)

    peers = [at_y(d) for d in (1, 2, 3)] + [at_x(d) for d in (1, 2, 3)] + [at_z(d) for d in range(1, 8)]
    peers += [at_core, at_next, at_prev]
    barrier = pltpu.get_barrier_semaphore()
    for peer in peers:
        pl.semaphore_signal(barrier, inc=1, device_id=peer, device_id_type=MESH)

    def load(src, dst, sem):
        copy = pltpu.make_async_copy(src, dst, sem)
        copy.start()
        return copy

    loads = [load(wq_hbm, wq_s, load_w.at[0]),
             load(wo_hbm, wcat_s.at[0], load_w.at[1]),
             load(text_hbm, text_s.at[pl.ds(WINDOW, S_DEV)], load_w.at[2]),
             load(wk_hbm, wk_s, load_w.at[3]),
             load(wv_hbm, wv_s, load_w.at[4])]

    def chunk(j, which):
        rows = pl.ds(pl.multiple_of(((head + 1 + j) % 4) * TILE, TILE), TILE)
        if which == 0:
            return pltpu.make_async_copy(frames_hbm.at[rows], frames_s.at[rows], load_f.at[j])
        return pltpu.make_async_copy(cot_hbm.at[rows], cot_s.at[rows], load_c.at[j])

    for j in range(4):
        chunk(j, 0).start()
        chunk(j, 1).start()

    loads[0].wait()
    wcat_s[1] = jnp.transpose(wq_s[...])
    loads[1].wait()

    def remote(src, dst, sends, recvs, index, peer):
        return pltpu.make_async_remote_copy(src_ref=src, dst_ref=dst, send_sem=sends.at[index], recv_sem=recvs.at[index],
                                            device_id=peer, device_id_type=MESH)

    def send(*args):
        copy = remote(*args)
        copy.start()
        return copy

    pl.semaphore_wait(barrier, len(peers))
    halo = [send(text_hbm.at[pl.ds(S_DEV - WINDOW, WINDOW)], text_s.at[pl.ds(0, WINDOW)], send_h, recv_h, 0, at_next),
            send(text_hbm.at[pl.ds(0, WINDOW)], text_s.at[pl.ds(WINDOW + S_DEV, WINDOW)], send_h, recv_h, 1, at_prev)]
    quarter = pl.ds(pl.multiple_of(x * 64, 64), 64)
    from_y = [send(wcat_s.at[core, quarter], wall_s.at[head, core, quarter], send_wy, recv_wy, d - 1, at_y(d)) for d in (1, 2, 3)]

    length = dur_ref[...]
    before = lax.broadcasted_iota(jnp.int32, (S_DEV, S_DEV), 1) <= lax.broadcasted_iota(jnp.int32, (S_DEV, S_DEV), 0)
    ends_s[...] = jnp.sum(jnp.where(before, jnp.broadcast_to(length, (S_DEV, S_DEV)), 0), axis=1, keepdims=True)
    gk_s[...] = jnp.zeros_like(gk_s)
    gv_s[...] = jnp.zeros_like(gv_s)
    for copy in loads[2:]:
        copy.wait()
    for copy in halo:
        copy.wait()
    keys = mm(text_s[...], wk_s[...], NN).astype(BF)
    vals = mm(text_s[...], wv_s[...], NN).astype(BF)
    for h in range(HEADS):
        k_s[h] = keys[:, h * HEAD_DIM:(h + 1) * HEAD_DIM]
        v_s[h] = vals[:, h * HEAD_DIM:(h + 1) * HEAD_DIM]
    first = jnp.where(seq == 0, WINDOW, 0)
    last = EXT - 1 - jnp.where(seq == RANGES - 1, WINDOW, 0)

    def exchange(j, which):
        lanes = pl.ds(pl.multiple_of(((head + 1 + j) % 4) * TILE, TILE), TILE)
        peer = (seq, (head + 1 + j) % 4)
        if which == 0:
            return remote(att_s.at[:, lanes], far_att.at[j], send_a, recv_a, j, peer)
        return remote(dq_s.at[:, lanes], far_dq.at[j], send_b, recv_b, j, peer)

    from_x = []
    for d in (1, 2, 3):
        source = (head + 4 - d) % 4
        for e in (1, 2, 3):
            place = wall_s.at[source, core, quarter]
            from_x.append(remote(place, place, send_wx, recv_wx, (d - 1) * 3 + e - 1, at_x(e)))

    @pl.loop(0, 8)
    def _(i):
        j = i // 2
        tile = ((head + 1 + j) % 4) * 2 + i % 2

        @pl.when(i % 2 == 0)
        def _():
            chunk(j, 0).wait()
            chunk(j, 1).wait()

        rows = pl.ds(pl.multiple_of(tile * SUB, SUB), SUB)
        qt_s[...] = mm(wcat_s[1], frames_s[rows, :], NT).astype(BF)
        ut_s[...] = mm(wcat_s[0], cot_s[rows, :], NT).astype(BF)

        @pl.when(i == 0)
        def _():
            for d in range(3):
                from_y[d].wait()
            for copy in from_x:
                copy.start()

        start = pl.multiple_of((tile // 2) * 16, 16)
        here = pl.ds(start, SPAN)
        position = lax.broadcasted_iota(jnp.int32, (S_DEV, SUB), 1) + tile * SUB
        own = jnp.sum((ends_s[...] <= position).astype(jnp.int32), axis=0, keepdims=True)
        low = jnp.maximum(own, first)
        high = jnp.minimum(own + 2 * WINDOW, last)
        state = lax.broadcasted_iota(jnp.int32, (SPAN, SUB), 0) + start
        allowed = (state >= low) & (state <= high)
        hs = range(HEADS)
        cols = [pl.ds(h * HEAD_DIM, HEAD_DIM) for h in hs]
        q = [qt_s[cols[h], :] for h in hs]
        u = [ut_s[cols[h], :] for h in hs]
        k = [k_s[h, here, :] for h in hs]
        v = [v_s[h, here, :] for h in hs]
        s = [jnp.where(allowed, mm(k[h], q[h], NN), -jnp.inf) for h in hs]
        dp = [mm(v[h], u[h], NN) for h in hs]
        e = [jnp.exp2((s[h] - jnp.max(s[h], axis=0, keepdims=True)) * (LOG2E * HEAD_DIM ** -0.5)) for h in hs]
        p = [e[h] * (1.0 / jnp.sum(e[h], axis=0, keepdims=True)) for h in hs]
        pb = [p[h].astype(BF) for h in hs]
        att = [mm(v[h], pb[h], TN).astype(BF) for h in hs]
        for h in hs:
            att_s[cols[h], rows] = att[h]
        delta = [jnp.sum(u[h].astype(F32) * att[h].astype(F32), axis=0, keepdims=True) for h in hs]
        ds = [(p[h] * (dp[h] - delta[h]) * HEAD_DIM ** -0.5).astype(BF) for h in hs]
        for h in hs:
            gv_s[h, here, :] += mm(pb[h], u[h], NT)
        for h in hs:
            dq_s[cols[h], rows] = mm(k[h], ds[h], TN).astype(BF)
        for h in hs:
            gk_s[h, here, :] += mm(ds[h], q[h], NT)

        @pl.when((i % 2 == 1) & (i < 6))
        def _():
            exchange(j, 0).start()
            exchange(j, 1).start()

    for h in range(HEADS):
        cols = slice(h * HEAD_DIM, (h + 1) * HEAD_DIM)
        later = slice(COLS + h * HEAD_DIM, COLS + (h + 1) * HEAD_DIM)
        edge_s[0, :, cols] = gk_s[h, :WINDOW].astype(BF)
        edge_s[1, :, cols] = gk_s[h, WINDOW + S_DEV:].astype(BF)
        edge_s[0, :, later] = gv_s[h, :WINDOW].astype(BF)
        edge_s[1, :, later] = gv_s[h, WINDOW + S_DEV:].astype(BF)
    edge_copies = [send(edge_s.at[0], far_edge.at[0], send_e, recv_e, 0, at_prev),
                   send(edge_s.at[1], far_edge.at[1], send_e, recv_e, 1, at_next)]

    def put(group, value, block):
        for part in range(2):
            for chip in range(4):
                for side in range(2):
                    at = part * 128 + chip * 32 + side * 16
                    term_s[group, side, chip, block * 2 + part, :, :] = value[at:at + 16]

    def frame_term(group, left_s, right_s):
        @pl.loop(0, 4)
        def _(block):
            lanes = pl.ds(pl.multiple_of(block * 256, 256), 256)
            value = mm(left_s[...], right_s[:, lanes], NN)
            put(group, jnp.transpose(value).astype(BF), block)

    def core_send(group):
        return send(term_s.at[group, 1 - core], near_s.at[group], send_c, recv_c, group, at_core)

    frame_term(0, att_s, cot_s)
    core_copies = [core_send(0)]
    frame_term(1, dq_s, frames_s)
    core_copies.append(core_send(1))
    for copy in edge_copies:
        copy.wait()
    inner = slice(WINDOW, WINDOW + S_DEV)
    for h in range(HEADS):
        for at, grad in ((h * HEAD_DIM, gk_s), (COLS + h * HEAD_DIM, gv_s)):
            cols = slice(at, at + HEAD_DIM)
            grad[h, WINDOW:2 * WINDOW] += far_edge[1, :, cols].astype(F32)
            grad[h, S_DEV:WINDOW + S_DEV] += far_edge[0, :, cols].astype(F32)
            kv_s[:, cols] = grad[h, inner].astype(BF)

    for which in range(2):
        @pl.loop(0, 4)
        def _(block):
            lanes = pl.ds(pl.multiple_of(block * 256, 256), 256)
            value = mm(text_s[inner, lanes], kv_s[:, which * COLS:(which + 1) * COLS], TN)
            put(2 + which, value.astype(BF), block)
        core_copies.append(core_send(2 + which))

    for part in range(4):
        rows = slice(part * 64, part * 64 + 64)
        value = mm(kv_s[rows, :COLS], wk_s[...], NT) + mm(kv_s[rows, COLS:], wv_s[...], NT)
        tterm_s[part] = value.astype(BF)
    text_copies = [send(tterm_s.at[y_of(d)], far_t.at[d - 1], send_t, recv_t, d - 1, at_y(d)) for d in (2, 1, 3)]

    for copy in from_x:
        copy.wait()
    from_core = []
    for d in (1, 2, 3):
        place = wall_s.at[(head + 4 - d) % 4, core]
        from_core.append(send(place, place, send_wc, recv_wc, d - 1, at_core))

    x_copies = []
    for group in range(4):
        core_copies[group].wait()

        @pl.loop(0, 4)
        def _(chip):
            sum_c[group, chip] = (term_s[group, core, chip].astype(F32) + near_s[group, chip].astype(F32)).astype(BF)
        x_copies.append([send(sum_c.at[group, x_of(d)], far_x.at[group, d - 1], send_x, recv_x, group * 3 + d - 1, at_x(d))
                         for d in (2, 1, 3)])

    def project(mine_s, far, which, out_ref):
        mine = pl.ds(pl.multiple_of(head * TILE, TILE), TILE)
        parts = [jnp.transpose(mine_s[:, mine])] + [jnp.transpose(far[d - 1]) for d in (1, 2, 3)]
        for block in range(4):
            lanes = slice(block * 256, block * 256 + 256)
            total = mm(parts[0], wcat_s[which, :, lanes], NN).astype(BF).astype(F32)
            for d in (1, 2, 3):
                total = total + mm(parts[d], wall_s[(head + 4 - d) % 4, which, :, lanes], NN).astype(BF).astype(F32)
            out_ref[:, lanes] = total.astype(BF)

    for copy in from_core:
        copy.wait()
    for j in range(3):
        exchange(j, 0).wait()
    project(att_s, far_att, 0, layer_ref)
    for j in range(3):
        exchange(j, 1).wait()
    project(dq_s, far_dq, 1, fgrad_ref)

    z_copies = []
    for group in range(4):
        for copy in x_copies[group]:
            copy.wait()
        total = sum_c[group, x].astype(F32)
        for d in range(3):
            total = total + far_x[group, d].astype(F32)
        sum_x[group] = total.astype(BF)
        z_copies.append([send(sum_x.at[group, z_of(d)], far_z.at[group, d - 1], send_z, recv_z, group * 7 + d - 1, at_z(d))
                         for d in (4, 3, 5, 2, 6, 1, 7)])

    for copy in text_copies:
        copy.wait()
    total = tterm_s[head].astype(F32)
    for d in range(3):
        total = total + far_t[d].astype(F32)
    tgrad_ref[...] = total.astype(BF)

    for group in range(4):
        for copy in z_copies[group]:
            copy.wait()
        total = sum_x[group, z].astype(F32)
        for d in range(7):
            total = total + far_z[group, d].astype(F32)
        wgrad_ref[group] = total


def on_device(frames, text_states, durations, w_query, w_key, w_value, w_out, cotangent):
    vmem = pl.BlockSpec(memory_space=pltpu.VMEM)
    hbm = pl.BlockSpec(memory_space=pl.ANY)
    dma = pltpu.SemaphoreType.DMA
    layer, fgrad, tgrad, wgrad = pl.pallas_call(
        kernel,
        in_specs=[hbm] * 3 + [vmem] + [hbm] * 4,
        out_specs=[vmem] * 4,
        out_shape=[
            jax.ShapeDtypeStruct((TILE, D), BF),
            jax.ShapeDtypeStruct((TILE, D), BF),
            jax.ShapeDtypeStruct((64, D), BF),
            jax.ShapeDtypeStruct((4, 16, COLS), F32),
        ],
        scratch_shapes=[
            pltpu.VMEM((F_DEV, D), BF),
            pltpu.VMEM((F_DEV, D), BF),
            pltpu.VMEM((EXT, D), BF),
            pltpu.VMEM((D, COLS), BF),
            pltpu.VMEM((D, COLS), BF),
            pltpu.VMEM((D, COLS), BF),
            pltpu.VMEM((2, COLS, D), BF),
            pltpu.VMEM((4, 2, COLS, D), BF),
            pltpu.VMEM((HEADS, EXT, HEAD_DIM), BF),
            pltpu.VMEM((HEADS, EXT, HEAD_DIM), BF),
            pltpu.VMEM((COLS, SUB), BF),
            pltpu.VMEM((COLS, SUB), BF),
            pltpu.VMEM((HEADS, EXT, HEAD_DIM), F32),
            pltpu.VMEM((HEADS, EXT, HEAD_DIM), F32),
            pltpu.VMEM((S_DEV, 1), jnp.int32),
            pltpu.VMEM((COLS, F_DEV), BF),
            pltpu.VMEM((COLS, F_DEV), BF),
            pltpu.VMEM((3, COLS, TILE), BF),
            pltpu.VMEM((3, COLS, TILE), BF),
            pltpu.VMEM((2, WINDOW, 2 * COLS), BF),
            pltpu.VMEM((2, WINDOW, 2 * COLS), BF),
            pltpu.VMEM((S_DEV, 2 * COLS), BF),
            pltpu.VMEM((4, 2, 4, 8, 16, COLS), BF),
            pltpu.VMEM((4, 4, 8, 16, COLS), BF),
            pltpu.VMEM((4, 4, 8, 16, COLS), BF),
            pltpu.VMEM((4, 3, 8, 16, COLS), BF),
            pltpu.VMEM((4, 8, 16, COLS), BF),
            pltpu.VMEM((4, 7, 16, COLS), BF),
            pltpu.VMEM((4, 64, D), BF),
            pltpu.VMEM((3, 64, D), BF),
            dma((5,)), dma((4,)), dma((4,)),
            dma((2,)), dma((2,)), dma((3,)), dma((3,)), dma((9,)), dma((9,)), dma((3,)), dma((3,)),
            dma((3,)), dma((3,)), dma((3,)), dma((3,)), dma((2,)), dma((2,)), dma((4,)), dma((4,)),
            dma((12,)), dma((12,)), dma((28,)), dma((28,)), dma((3,)), dma((3,)),
        ],
        compiler_params=pltpu.CompilerParams(collective_id=0, has_side_effects=True, vmem_limit_bytes=60 * 2 ** 20),
        cost_estimate=pl.CostEstimate(flops=15 * 10 ** 9, bytes_accessed=16 * 10 ** 6, transcendentals=3 * 10 ** 6),
    )(frames, cotangent, text_states, durations, w_query, w_key, w_value, w_out)
    return layer, fgrad, tgrad, wgrad[1], wgrad[2], wgrad[3], jnp.transpose(wgrad[0])


def solution(mesh):
    placed = (
        P("seq", None),
        P("seq", None),
        P("seq", None),
        P(None, "head"),
        P(None, "head"),
        P(None, "head"),
        P("head", None),
        P("seq", None),
    )
    return jax.shard_map(
        on_device,
        mesh=mesh,
        in_specs=placed,
        out_specs=(
            P(("seq", "head"), None),
            P(("seq", "head"), None),
            P(("seq", "head"), None),
            P("seq", "head"),
            P("seq", "head"),
            P("seq", "head"),
            P("head", "seq"),
        ),
        check_vma=False,
    )
```

time: 119 us -> 68.2 us (0.57)
  waiting for transfers between devices: 19.5 us -> 0 us
  between operations: 14.2 us -> 0.65 us
  local copies, waits for them, and re-layouts: 15.3 us -> 6.61 us
  other arithmetic: 4.43 us -> 0 us
  starting transfers between devices: 3.36 us -> 0 us
    all_gather x1 -> x0, waiting for transfers between devices: 14.2 us -> none  [on_device(): wall = lax.all_gather(jnp.concatenate([w_out, wqt], axis=0), 'head', axis=0)]
    unnamed x26 -> x5, local copies, waits for them, and re-layouts: 12.7 us -> 5.18 us
    ppermute x2 -> x0, waiting for transfers between devices: 5.31 us -> none  [the longest x1 5.19 us: on_device(): lax.ppermute(text_states[S_DEV - WINDOW:], 'seq', [(i, (i + 1) % RANGES)...]
    ppermute x2 -> x0, starting transfers between devices: 3.32 us -> none  [the longest x1 3.32 us: on_device(): lax.ppermute(text_states[:WINDOW], 'seq', [(i, (i - 1) % RANGES) for i in...]
    concatenate x2 -> x0, other arithmetic: 2.97 us -> none  [the longest x1 2.08 us: on_device(): wall = lax.all_gather(jnp.concatenate([w_out, wqt], axis=0), 'head', axis=0)]
    pallas_call x2 -> x1, Pallas kernels: 61.4 us -> 60.8 us  [on_device(): pl.pallas_call(kernel, in_specs=[hbm] * 3 + [vmem] + [hbm] * 4, out_specs...]
  transfers between devices with their start and end apart: 3 -> 0, of which waited for: 3 -> 0; matrix products, arithmetic and copies ran while one was open for 3% -> 0% of each run, Pallas kernels for 18% -> 0%
where the time goes in v2:
time: 68.2 us; the launch traced here: 68 us
  Pallas kernels  60.8 us (89%)
  local copies, waits for them, and re-layouts  6.61 us (10%)
    pallas_call x1, Pallas kernels, on_device(): pl.pallas_call(kernel, in_specs=[hbm] * 3 + [vmem] + [hbm] * 4, out_specs...  60.8 us
    unnamed x5, local copies, waits for them, and re-layouts  5.18 us
    transpose x1, local copies, waits for them, and re-layouts, on_device(): jnp.transpose(wgrad[0])  1.43 us

profile of v2, /device:TPU:1, one launch (start us, length us, event | category | flops | bytes accessed | tf_op | source)
XLA Modules:
  0.0 68.0 jit_solution(477807775276720565)
XLA Ops:
  0.6 60.8 %shard_map.135 = (bf16[512,1024]{1,0:T(8,128)(2,1)}, bf16[512,1024]{1,0:T(8,128)(2,1)}, bf16[64,1024]{1,0:T(8,128)(2,1)}, f32[4,16,256]{2,1,0:T(8,128)}) custom-call(bf16[2048,1024]{1,0:T(8,128)(2,1)} %frames_hbm.1, bf16[2048,1024]{1,0:T(8,128)(2,1)} %cot_hbm.1, bf16[256,1024]{1,0:T(8,128)(2,1)} %text_hbm.1, s32[1,256]{1,0:T(1,128)} %dur_ref.1, ...), custom_call_target="tpu_custom_call" | custom-call | flops 15000000512 | bytes 16000000 | tf_op jit(solution)/shard_map/pallas_call | solution.py:309
  61.4 0.0 copy-start
  61.4 1.4 %slice_bitcast_fusion = (f32[256,16]{0,1:T(8,128)}, f32[16,256]{1,0:T(8,128)}, f32[16,256]{1,0:T(8,128)}, f32[16,256]{1,0:T(8,128)}) fusion(f32[4,16,256]{2,1,0:T(8,128)} %get-tuple-element.14), kind=kLoop, calls=%fused_computation | loop fusion | bytes 131072 | tf_op jit(solution)/shard_map/transpose | solution.py:358
  62.8 2.3 %copy.18 = bf16[512,1024]{1,0:T(8,128)(2,1)} copy(bf16[512,1024]{1,0:T(8,128)(2,1)} %get-tuple-element.26) | data formatting | bytes 2097152
  65.1 2.3 %copy.19 = bf16[512,1024]{1,0:T(8,128)(2,1)} copy(bf16[512,1024]{1,0:T(8,128)(2,1)} %get-tuple-element.27) | data formatting | bytes 2097152
  67.4 0.0 copy-done
  67.4 0.7 copy.20
Async XLA Ops:
  61.4 6.0 %copy-start = (bf16[64,1024]{1,0:T(8,128)(2,1)S(1)}, bf16[64,1024]{1,0:T(8,128)(2,1)}, u32[]{:S(2)}) copy-start(bf16[64,1024]{1,0:T(8,128)(2,1)} %get-tuple-element.28) | copy-start | bytes 393220

commit v3 on v2

--- a/solution.py
+++ b/solution.py
@@ -31,11 +31,12 @@
 
 
 def kernel(frames_hbm, cot_hbm, text_hbm, dur_ref, wq_hbm, wk_hbm, wv_hbm, wo_hbm,
-           layer_ref, fgrad_ref, tgrad_ref, wgrad_ref,
+           layer_hbm, fgrad_hbm, tgrad_hbm, wgrad_hbm,
+           layer_s, fgrad_s, tgrad_s, wgrad_s,
            frames_s, cot_s, text_s, wq_s, wk_s, wv_s, wcat_s, wall_s,
            k_s, v_s, qt_s, ut_s, gk_s, gv_s, ends_s, att_s, dq_s,
            far_att, far_dq, edge_s, far_edge, kv_s, term_s, near_s, sum_c, far_x, sum_x, far_z, tterm_s, far_t,
-           load_w, load_f, load_c,
+           load_w, load_f, load_c, store_sem,
            send_h, recv_h, send_wy, recv_wy, send_wx, recv_wx, send_wc, recv_wc,
            send_a, recv_a, send_b, recv_b, send_e, recv_e, send_c, recv_c, send_x, recv_x, send_z, recv_z, send_t, recv_t):
     seq, head = lax.axis_index("seq"), lax.axis_index("head")
@@ -96,6 +97,14 @@
     quarter = pl.ds(pl.multiple_of(x * 64, 64), 64)
     from_y = [send(wcat_s.at[core, quarter], wall_s.at[head, core, quarter], send_wy, recv_wy, d - 1, at_y(d)) for d in (1, 2, 3)]
 
+    @pl.loop(0, 4)
+    def _(j):
+        chunk(j, 0).wait()
+        chunk(j, 1).wait()
+        rows = pl.ds(pl.multiple_of(((head + 1 + j) % 4) * TILE, TILE), TILE)
+        qt_s[:, rows] = mm(wcat_s[1], frames_s[rows, :], NT).astype(BF)
+        ut_s[:, rows] = mm(wcat_s[0], cot_s[rows, :], NT).astype(BF)
+
     length = dur_ref[...]
     before = lax.broadcasted_iota(jnp.int32, (S_DEV, S_DEV), 1) <= lax.broadcasted_iota(jnp.int32, (S_DEV, S_DEV), 0)
     ends_s[...] = jnp.sum(jnp.where(before, jnp.broadcast_to(length, (S_DEV, S_DEV)), 0), axis=1, keepdims=True)
@@ -113,41 +122,27 @@
     first = jnp.where(seq == 0, WINDOW, 0)
     last = EXT - 1 - jnp.where(seq == RANGES - 1, WINDOW, 0)
 
-    def exchange(j, which):
-        lanes = pl.ds(pl.multiple_of(((head + 1 + j) % 4) * TILE, TILE), TILE)
-        peer = (seq, (head + 1 + j) % 4)
+    def exchange(i, which):
+        lanes = pl.ds(pl.multiple_of(((head + 1 + i // 2) % 4) * TILE + (i % 2) * SUB, SUB), SUB)
+        there = pl.ds(pl.multiple_of((i % 2) * SUB, SUB), SUB)
+        peer = (seq, (head + 1 + i // 2) % 4)
         if which == 0:
-            return remote(att_s.at[:, lanes], far_att.at[j], send_a, recv_a, j, peer)
-        return remote(dq_s.at[:, lanes], far_dq.at[j], send_b, recv_b, j, peer)
+            return remote(att_s.at[:, lanes], far_att.at[i // 2, :, there], send_a, recv_a, i, peer)
+        return remote(dq_s.at[:, lanes], far_dq.at[i // 2, :, there], send_b, recv_b, i, peer)
 
     from_x = []
     for d in (1, 2, 3):
         source = (head + 4 - d) % 4
+        from_y[d - 1].wait()
         for e in (1, 2, 3):
             place = wall_s.at[source, core, quarter]
-            from_x.append(remote(place, place, send_wx, recv_wx, (d - 1) * 3 + e - 1, at_x(e)))
+            from_x.append(send(place, place, send_wx, recv_wx, (d - 1) * 3 + e - 1, at_x(e)))
 
     @pl.loop(0, 8)
     def _(i):
-        j = i // 2
-        tile = ((head + 1 + j) % 4) * 2 + i % 2
-
-        @pl.when(i % 2 == 0)
-        def _():
-            chunk(j, 0).wait()
-            chunk(j, 1).wait()
+        tile = ((head + 1 + i // 2) % 4) * 2 + i % 2
 
         rows = pl.ds(pl.multiple_of(tile * SUB, SUB), SUB)
-        qt_s[...] = mm(wcat_s[1], frames_s[rows, :], NT).astype(BF)
-        ut_s[...] = mm(wcat_s[0], cot_s[rows, :], NT).astype(BF)
-
-        @pl.when(i == 0)
-        def _():
-            for d in range(3):
-                from_y[d].wait()
-            for copy in from_x:
-                copy.start()
-
         start = pl.multiple_of((tile // 2) * 16, 16)
         here = pl.ds(start, SPAN)
         position = lax.broadcasted_iota(jnp.int32, (S_DEV, SUB), 1) + tile * SUB
@@ -158,8 +153,8 @@
         allowed = (state >= low) & (state <= high)
         hs = range(HEADS)
         cols = [pl.ds(h * HEAD_DIM, HEAD_DIM) for h in hs]
-        q = [qt_s[cols[h], :] for h in hs]
-        u = [ut_s[cols[h], :] for h in hs]
+        q = [qt_s[cols[h], rows] for h in hs]
+        u = [ut_s[cols[h], rows] for h in hs]
         k = [k_s[h, here, :] for h in hs]
         v = [v_s[h, here, :] for h in hs]
         s = [jnp.where(allowed, mm(k[h], q[h], NN), -jnp.inf) for h in hs]
@@ -179,10 +174,10 @@
         for h in hs:
             gk_s[h, here, :] += mm(ds[h], q[h], NT)
 
-        @pl.when((i % 2 == 1) & (i < 6))
+        @pl.when(i < 6)
         def _():
-            exchange(j, 0).start()
-            exchange(j, 1).start()
+            exchange(i, 0).start()
+            exchange(i, 1).start()
 
     for h in range(HEADS):
         cols = slice(h * HEAD_DIM, (h + 1) * HEAD_DIM)
@@ -211,6 +206,17 @@
     def core_send(group):
         return send(term_s.at[group, 1 - core], near_s.at[group], send_c, recv_c, group, at_core)
 
+    x_copies = []
+
+    def chip_sum(group):
+        core_copies[group].wait()
+
+        @pl.loop(0, 4)
+        def _(chip):
+            sum_c[group, chip] = (term_s[group, core, chip].astype(F32) + near_s[group, chip].astype(F32)).astype(BF)
+        x_copies.append([send(sum_c.at[group, x_of(d)], far_x.at[group, d - 1], send_x, recv_x, group * 3 + d - 1, at_x(d))
+                         for d in (2, 1, 3)])
+
     frame_term(0, att_s, cot_s)
     core_copies = [core_send(0)]
     frame_term(1, dq_s, frames_s)
@@ -224,6 +230,7 @@
             grad[h, WINDOW:2 * WINDOW] += far_edge[1, :, cols].astype(F32)
             grad[h, S_DEV:WINDOW + S_DEV] += far_edge[0, :, cols].astype(F32)
             kv_s[:, cols] = grad[h, inner].astype(BF)
+    chip_sum(0)
 
     for which in range(2):
         @pl.loop(0, 4)
@@ -232,12 +239,15 @@
             value = mm(text_s[inner, lanes], kv_s[:, which * COLS:(which + 1) * COLS], TN)
             put(2 + which, value.astype(BF), block)
         core_copies.append(core_send(2 + which))
+    chip_sum(1)
 
     for part in range(4):
         rows = slice(part * 64, part * 64 + 64)
         value = mm(kv_s[rows, :COLS], wk_s[...], NT) + mm(kv_s[rows, COLS:], wv_s[...], NT)
         tterm_s[part] = value.astype(BF)
     text_copies = [send(tterm_s.at[y_of(d)], far_t.at[d - 1], send_t, recv_t, d - 1, at_y(d)) for d in (2, 1, 3)]
+    chip_sum(2)
+    chip_sum(3)
 
     for copy in from_x:
         copy.wait()
@@ -245,35 +255,6 @@
     for d in (1, 2, 3):
         place = wall_s.at[(head + 4 - d) % 4, core]
         from_core.append(send(place, place, send_wc, recv_wc, d - 1, at_core))
-
-    x_copies = []
-    for group in range(4):
-        core_copies[group].wait()
-
-        @pl.loop(0, 4)
-        def _(chip):
-            sum_c[group, chip] = (term_s[group, core, chip].astype(F32) + near_s[group, chip].astype(F32)).astype(BF)
-        x_copies.append([send(sum_c.at[group, x_of(d)], far_x.at[group, d - 1], send_x, recv_x, group * 3 + d - 1, at_x(d))
-                         for d in (2, 1, 3)])
-
-    def project(mine_s, far, which, out_ref):
-        mine = pl.ds(pl.multiple_of(head * TILE, TILE), TILE)
-        parts = [jnp.transpose(mine_s[:, mine])] + [jnp.transpose(far[d - 1]) for d in (1, 2, 3)]
-        for block in range(4):
-            lanes = slice(block * 256, block * 256 + 256)
-            total = mm(parts[0], wcat_s[which, :, lanes], NN).astype(BF).astype(F32)
-            for d in (1, 2, 3):
-                total = total + mm(parts[d], wall_s[(head + 4 - d) % 4, which, :, lanes], NN).astype(BF).astype(F32)
-            out_ref[:, lanes] = total.astype(BF)
-
-    for copy in from_core:
-        copy.wait()
-    for j in range(3):
-        exchange(j, 0).wait()
-    project(att_s, far_att, 0, layer_ref)
-    for j in range(3):
-        exchange(j, 1).wait()
-    project(dq_s, far_dq, 1, fgrad_ref)
 
     z_copies = []
     for group in range(4):
@@ -286,12 +267,34 @@
         z_copies.append([send(sum_x.at[group, z_of(d)], far_z.at[group, d - 1], send_z, recv_z, group * 7 + d - 1, at_z(d))
                          for d in (4, 3, 5, 2, 6, 1, 7)])
 
+    def project(mine_s, far, which, out_s):
+        mine = pl.ds(pl.multiple_of(head * TILE, TILE), TILE)
+        parts = [jnp.transpose(mine_s[:, mine])] + [jnp.transpose(far[d - 1]) for d in (1, 2, 3)]
+        for block in range(4):
+            lanes = slice(block * 256, block * 256 + 256)
+            total = mm(parts[0], wcat_s[which, :, lanes], NN).astype(BF).astype(F32)
+            for d in (1, 2, 3):
+                total = total + mm(parts[d], wall_s[(head + 4 - d) % 4, which, :, lanes], NN).astype(BF).astype(F32)
+            out_s[:, lanes] = total.astype(BF)
+
+    for copy in from_core:
+        copy.wait()
+    for i in range(6):
+        exchange(i, 0).wait()
+    project(att_s, far_att, 0, layer_s)
+    stores = [load(layer_s, layer_hbm, store_sem.at[0])]
+    for i in range(6):
+        exchange(i, 1).wait()
+    project(dq_s, far_dq, 1, fgrad_s)
+    stores.append(load(fgrad_s, fgrad_hbm, store_sem.at[1]))
+
     for copy in text_copies:
         copy.wait()
     total = tterm_s[head].astype(F32)
     for d in range(3):
         total = total + far_t[d].astype(F32)
-    tgrad_ref[...] = total.astype(BF)
+    tgrad_s[...] = total.astype(BF)
+    stores.append(load(tgrad_s, tgrad_hbm, store_sem.at[2]))
 
     for group in range(4):
         for copy in z_copies[group]:
@@ -299,17 +302,41 @@
         total = sum_x[group, z].astype(F32)
         for d in range(7):
             total = total + far_z[group, d].astype(F32)
-        wgrad_ref[group] = total
+        wgrad_s[group] = total
+    stores.append(load(wgrad_s, wgrad_hbm, store_sem.at[3]))
+    for copy in stores:
+        copy.wait()
+
+
+def move_kernel(layer_in, fgrad_in, tgrad_in, wgrad_in, layer_out, fgrad_out, tgrad_out, w0, w1, w2, w3,
+                layer_s, fgrad_s, tgrad_s, wgrad_s, into, out_of):
+    pieces = []
+    for part in range(4):
+        rows = pl.ds(part * 128, 128)
+        pieces.append((layer_in.at[rows], layer_s.at[rows], layer_out.at[rows]))
+        pieces.append((fgrad_in.at[rows], fgrad_s.at[rows], fgrad_out.at[rows]))
+    pieces.append((tgrad_in, tgrad_s, tgrad_out))
+    for group, out in enumerate((w0, w1, w2, w3)):
+        pieces.append((wgrad_in.at[group], wgrad_s.at[group], out))
+    reads = [pltpu.make_async_copy(src, mid, into.at[n]) for n, (src, mid, _) in enumerate(pieces)]
+    writes = [pltpu.make_async_copy(mid, dst, out_of.at[n]) for n, (_, mid, dst) in enumerate(pieces)]
+    for copy in reads:
+        copy.start()
+    for read, write in zip(reads, writes):
+        read.wait()
+        write.start()
+    for copy in writes:
+        copy.wait()
 
 
 def on_device(frames, text_states, durations, w_query, w_key, w_value, w_out, cotangent):
     vmem = pl.BlockSpec(memory_space=pltpu.VMEM)
-    hbm = pl.BlockSpec(memory_space=pl.ANY)
+    hbm = pl.BlockSpec(memory_space=pltpu.HBM)
     dma = pltpu.SemaphoreType.DMA
     layer, fgrad, tgrad, wgrad = pl.pallas_call(
         kernel,
         in_specs=[hbm] * 3 + [vmem] + [hbm] * 4,
-        out_specs=[vmem] * 4,
+        out_specs=[hbm] * 4,
         out_shape=[
             jax.ShapeDtypeStruct((TILE, D), BF),
             jax.ShapeDtypeStruct((TILE, D), BF),
@@ -317,6 +344,10 @@
             jax.ShapeDtypeStruct((4, 16, COLS), F32),
         ],
         scratch_shapes=[
+            pltpu.VMEM((TILE, D), BF),
+            pltpu.VMEM((TILE, D), BF),
+            pltpu.VMEM((64, D), BF),
+            pltpu.VMEM((4, 16, COLS), F32),
             pltpu.VMEM((F_DEV, D), BF),
             pltpu.VMEM((F_DEV, D), BF),
             pltpu.VMEM((EXT, D), BF),
@@ -327,8 +358,8 @@
             pltpu.VMEM((4, 2, COLS, D), BF),
             pltpu.VMEM((HEADS, EXT, HEAD_DIM), BF),
             pltpu.VMEM((HEADS, EXT, HEAD_DIM), BF),
-            pltpu.VMEM((COLS, SUB), BF),
-            pltpu.VMEM((COLS, SUB), BF),
+            pltpu.VMEM((COLS, F_DEV), BF),
+            pltpu.VMEM((COLS, F_DEV), BF),
             pltpu.VMEM((HEADS, EXT, HEAD_DIM), F32),
             pltpu.VMEM((HEADS, EXT, HEAD_DIM), F32),
             pltpu.VMEM((S_DEV, 1), jnp.int32),
@@ -347,15 +378,36 @@
             pltpu.VMEM((4, 7, 16, COLS), BF),
             pltpu.VMEM((4, 64, D), BF),
             pltpu.VMEM((3, 64, D), BF),
-            dma((5,)), dma((4,)), dma((4,)),
+            dma((5,)), dma((4,)), dma((4,)), dma((4,)),
             dma((2,)), dma((2,)), dma((3,)), dma((3,)), dma((9,)), dma((9,)), dma((3,)), dma((3,)),
-            dma((3,)), dma((3,)), dma((3,)), dma((3,)), dma((2,)), dma((2,)), dma((4,)), dma((4,)),
+            dma((6,)), dma((6,)), dma((6,)), dma((6,)), dma((2,)), dma((2,)), dma((4,)), dma((4,)),
             dma((12,)), dma((12,)), dma((28,)), dma((28,)), dma((3,)), dma((3,)),
         ],
         compiler_params=pltpu.CompilerParams(collective_id=0, has_side_effects=True, vmem_limit_bytes=60 * 2 ** 20),
         cost_estimate=pl.CostEstimate(flops=15 * 10 ** 9, bytes_accessed=16 * 10 ** 6, transcendentals=3 * 10 ** 6),
     )(frames, cotangent, text_states, durations, w_query, w_key, w_value, w_out)
-    return layer, fgrad, tgrad, wgrad[1], wgrad[2], wgrad[3], jnp.transpose(wgrad[0])
+    small = jax.ShapeDtypeStruct((16, COLS), F32)
+    layer, fgrad, tgrad, w0, w1, w2, w3 = pl.pallas_call(
+        move_kernel,
+        in_specs=[hbm] * 4,
+        out_specs=[hbm] * 7,
+        out_shape=[
+            jax.ShapeDtypeStruct((TILE, D), BF),
+            jax.ShapeDtypeStruct((TILE, D), BF),
+            jax.ShapeDtypeStruct((64, D), BF),
+            small, small, small, small,
+        ],
+        scratch_shapes=[
+            pltpu.VMEM((TILE, D), BF),
+            pltpu.VMEM((TILE, D), BF),
+            pltpu.VMEM((64, D), BF),
+            pltpu.VMEM((4, 16, COLS), F32),
+            dma((13,)), dma((13,)),
+        ],
+        compiler_params=pltpu.CompilerParams(vmem_limit_bytes=60 * 2 ** 20),
+        cost_estimate=pl.CostEstimate(flops=0, bytes_accessed=5 * 10 ** 6, transcendentals=0),
+    )(layer, fgrad, tgrad, wgrad)
+    return layer, fgrad, tgrad, w1, w2, w3, jnp.transpose(w0)
 
 
 def solution(mesh):

time: 68.2 us -> 57 us (0.84)
  local copies, waits for them, and re-layouts: 6.61 us -> 0 us
  Pallas kernels: 60.8 us -> 56.2 us
    pallas_call x1, Pallas kernels: 60.8 us -> 53.6 us  [on_device(): pl.pallas_call(kernel, in_specs=[hbm] * 3 + [vmem] + [hbm] * 4, out_specs...]
    unnamed x5 -> x0, local copies, waits for them, and re-layouts: 5.18 us -> none
    pallas_call x0 -> x1, Pallas kernels: none -> 2.53 us  [on_device(): pl.pallas_call(move_kernel, in_specs=[hbm] * 4, out_specs=[hbm] * 7, out_...]
    transpose x1 -> x0, local copies, waits for them, and re-layouts: 1.43 us -> none  [on_device(): jnp.transpose(wgrad[0])]
where the time goes in v3:
time: 57 us; the launch traced here: 56.8 us
  Pallas kernels  56.2 us (99%)
  between operations  0.64 us (1%)
    pallas_call x1, Pallas kernels, on_device(): pl.pallas_call(kernel, in_specs=[hbm] * 3 + [vmem] + [hbm] * 4, out_specs...  53.6 us
    pallas_call x1, Pallas kernels, on_device(): pl.pallas_call(move_kernel, in_specs=[hbm] * 4, out_specs=[hbm] * 7, out_...  2.53 us

profile of v3, /device:TPU:1, one launch (start us, length us, event | category | flops | bytes accessed | tf_op | source)
XLA Modules:
  0.0 56.8 jit_solution(5954014787022153052)
XLA Ops:
  0.6 53.6 %shard_map.135 = (bf16[512,1024]{1,0:T(8,128)(2,1)}, bf16[512,1024]{1,0:T(8,128)(2,1)}, bf16[64,1024]{1,0:T(8,128)(2,1)}, f32[4,16,256]{2,1,0:T(8,128)}) custom-call(bf16[2048,1024]{1,0:T(8,128)(2,1)} %frames_hbm.1, bf16[2048,1024]{1,0:T(8,128)(2,1)} %cot_hbm.1, bf16[256,1024]{1,0:T(8,128)(2,1)} %text_hbm.1, s32[1,256]{1,0:T(1,128)} %dur_ref.1, ...), custom_call_target="tpu_custom_call" | custom-call | flops 15000000512 | bytes 16000000 | tf_op jit(solution)/shard_map/pallas_call | solution.py:336
  54.3 2.5 %shard_map.136 = (bf16[512,1024]{1,0:T(8,128)(2,1)}, bf16[512,1024]{1,0:T(8,128)(2,1)}, bf16[64,1024]{1,0:T(8,128)(2,1)}, f32[16,256]{1,0:T(8,128)}, f32[16,256]...) custom-call(bf16[512,1024]{1,0:T(8,128)(2,1)} %get-tuple-element.18.layer_in, ...), custom_call_target="tpu_custom_call" | custom-call | bytes 5000000 | tf_op jit(solution)/shard_map/pallas_call | solution.py:390

commit v4 on v3

--- a/solution.py
+++ b/solution.py
@@ -35,9 +35,10 @@
            layer_s, fgrad_s, tgrad_s, wgrad_s,
            frames_s, cot_s, text_s, wq_s, wk_s, wv_s, wcat_s, wall_s,
            k_s, v_s, qt_s, ut_s, gk_s, gv_s, ends_s, att_s, dq_s,
-           far_att, far_dq, edge_s, far_edge, kv_s, term_s, near_s, sum_c, far_x, sum_x, far_z, tterm_s, far_t,
+           far_att, far_dq, edge_s, far_edge, kv_s, term_s, near_s, sum_c, far_x, sum_x, far_z,
+           tterm_s, far_t, sum_f,
            load_w, load_f, load_c, store_sem,
-           send_h, recv_h, send_wy, recv_wy, send_wx, recv_wx, send_wc, recv_wc,
+           send_h, recv_h, send_wy, recv_wy, send_wz, recv_wz, send_wx, recv_wx, send_wc, recv_wc,
            send_a, recv_a, send_b, recv_b, send_e, recv_e, send_c, recv_c, send_x, recv_x, send_z, recv_z, send_t, recv_t):
     seq, head = lax.axis_index("seq"), lax.axis_index("head")
     core, x, z = seq % 2, (seq // 2) % 4, seq // 8
@@ -69,7 +70,7 @@
              load(wv_hbm, wv_s, load_w.at[4])]
 
     def chunk(j, which):
-        rows = pl.ds(pl.multiple_of(((head + 1 + j) % 4) * TILE, TILE), TILE)
+        rows = pl.ds(pl.multiple_of(((head + jnp.where(j == 0, 2, jnp.where(j == 1, 1, jnp.where(j == 2, 3, 0)))) % 4) * TILE, TILE), TILE)
         if which == 0:
             return pltpu.make_async_copy(frames_hbm.at[rows], frames_s.at[rows], load_f.at[j])
         return pltpu.make_async_copy(cot_hbm.at[rows], cot_s.at[rows], load_c.at[j])
@@ -94,16 +95,23 @@
     pl.semaphore_wait(barrier, len(peers))
     halo = [send(text_hbm.at[pl.ds(S_DEV - WINDOW, WINDOW)], text_s.at[pl.ds(0, WINDOW)], send_h, recv_h, 0, at_next),
             send(text_hbm.at[pl.ds(0, WINDOW)], text_s.at[pl.ds(WINDOW + S_DEV, WINDOW)], send_h, recv_h, 1, at_prev)]
-    quarter = pl.ds(pl.multiple_of(x * 64, 64), 64)
-    from_y = [send(wcat_s.at[core, quarter], wall_s.at[head, core, quarter], send_wy, recv_wy, d - 1, at_y(d)) for d in (1, 2, 3)]
+    by_x = pl.ds(pl.multiple_of(x * 32, 32), 32)
+    by_z = pl.ds(pl.multiple_of(128 + z * 16, 16), 16)
+    from_y = []
+    for d in (1, 2, 3):
+        from_y.append(send(wcat_s.at[core, by_x], wall_s.at[d - 1, core, by_x], send_wy, recv_wy, d - 1, at_y(d)))
+        from_y.append(send(wcat_s.at[core, by_z], wall_s.at[d - 1, core, by_z], send_wy, recv_wy, d + 2, at_y(d)))
+
+    def projections(j):
+        chunk(j, 0).wait()
+        chunk(j, 1).wait()
+        rows = pl.ds(pl.multiple_of(((head + jnp.where(j == 0, 2, jnp.where(j == 1, 1, jnp.where(j == 2, 3, 0)))) % 4) * TILE, TILE), TILE)
+        qt_s[:, rows] = mm(wcat_s[1], frames_s[rows, :], NT).astype(BF)
+        ut_s[:, rows] = mm(wcat_s[0], cot_s[rows, :], NT).astype(BF)
 
     @pl.loop(0, 4)
     def _(j):
-        chunk(j, 0).wait()
-        chunk(j, 1).wait()
-        rows = pl.ds(pl.multiple_of(((head + 1 + j) % 4) * TILE, TILE), TILE)
-        qt_s[:, rows] = mm(wcat_s[1], frames_s[rows, :], NT).astype(BF)
-        ut_s[:, rows] = mm(wcat_s[0], cot_s[rows, :], NT).astype(BF)
+        projections(j)
 
     length = dur_ref[...]
     before = lax.broadcasted_iota(jnp.int32, (S_DEV, S_DEV), 1) <= lax.broadcasted_iota(jnp.int32, (S_DEV, S_DEV), 0)
@@ -122,25 +130,36 @@
     first = jnp.where(seq == 0, WINDOW, 0)
     last = EXT - 1 - jnp.where(seq == RANGES - 1, WINDOW, 0)
 
+    def place_of(i):
+        if isinstance(i, int):
+            return ((2, 0), (2, 1), (1, 0), (3, 0), (1, 1), (3, 1), (0, 0), (0, 1))[i]
+        middle = (i >= 2) & (i < 6)
+        d = jnp.where(middle, 1 + 2 * (i % 2), jnp.where(i < 2, 2, 0))
+        return d, jnp.where(middle, (i - 2) // 2, i % 2)
+
     def exchange(i, which):
-        lanes = pl.ds(pl.multiple_of(((head + 1 + i // 2) % 4) * TILE + (i % 2) * SUB, SUB), SUB)
-        there = pl.ds(pl.multiple_of((i % 2) * SUB, SUB), SUB)
-        peer = (seq, (head + 1 + i // 2) % 4)
+        d, part = place_of(i)
+        peer_y = (head + d) % 4
+        lanes = pl.ds(pl.multiple_of(peer_y * TILE + part * SUB, SUB), SUB)
+        there = pl.ds(pl.multiple_of(part * SUB, SUB), SUB)
         if which == 0:
-            return remote(att_s.at[:, lanes], far_att.at[i // 2, :, there], send_a, recv_a, i, peer)
-        return remote(dq_s.at[:, lanes], far_dq.at[i // 2, :, there], send_b, recv_b, i, peer)
-
-    from_x = []
-    for d in (1, 2, 3):
-        source = (head + 4 - d) % 4
-        from_y[d - 1].wait()
-        for e in (1, 2, 3):
-            place = wall_s.at[source, core, quarter]
-            from_x.append(send(place, place, send_wx, recv_wx, (d - 1) * 3 + e - 1, at_x(e)))
+            return remote(att_s.at[:, lanes], far_att.at[d - 1, :, there], send_a, recv_a, i, (seq, peer_y))
+        return remote(dq_s.at[:, lanes], far_dq.at[d - 1, :, there], send_b, recv_b, i, (seq, peer_y))
+
+    slot_x, slot_z = wall_s.at[:, core, by_x], wall_s.at[:, core, by_z]
+    from_x = [remote(slot_x, slot_x, send_wx, recv_wx, d - 1, at_x(d)) for d in (2, 1, 3)]
+    from_z = [remote(slot_z, slot_z, send_wz, recv_wz, d - 1, at_z(d)) for d in (4, 3, 5, 2, 6, 1, 7)]
 
     @pl.loop(0, 8)
     def _(i):
-        tile = ((head + 1 + i // 2) % 4) * 2 + i % 2
+        d, part = place_of(i)
+        tile = ((head + d) % 4) * 2 + part
+        @pl.when(i == 2)
+        def _():
+            for copy in from_y:
+                copy.wait()
+            for copy in from_z + from_x:
+                copy.start()
 
         rows = pl.ds(pl.multiple_of(tile * SUB, SUB), SUB)
         start = pl.multiple_of((tile // 2) * 16, 16)
@@ -177,7 +196,6 @@
         @pl.when(i < 6)
         def _():
             exchange(i, 0).start()
-            exchange(i, 1).start()
 
     for h in range(HEADS):
         cols = slice(h * HEAD_DIM, (h + 1) * HEAD_DIM)
@@ -188,6 +206,8 @@
         edge_s[1, :, later] = gv_s[h, WINDOW + S_DEV:].astype(BF)
     edge_copies = [send(edge_s.at[0], far_edge.at[0], send_e, recv_e, 0, at_prev),
                    send(edge_s.at[1], far_edge.at[1], send_e, recv_e, 1, at_next)]
+    for i in range(6):
+        exchange(i, 1).start()
 
     def put(group, value, block):
         for part in range(2):
@@ -206,7 +226,7 @@
     def core_send(group):
         return send(term_s.at[group, 1 - core], near_s.at[group], send_c, recv_c, group, at_core)
 
-    x_copies = []
+    x_copies, z_copies, core_copies = {}, {}, {}
 
     def chip_sum(group):
         core_copies[group].wait()
@@ -214,13 +234,37 @@
         @pl.loop(0, 4)
         def _(chip):
             sum_c[group, chip] = (term_s[group, core, chip].astype(F32) + near_s[group, chip].astype(F32)).astype(BF)
-        x_copies.append([send(sum_c.at[group, x_of(d)], far_x.at[group, d - 1], send_x, recv_x, group * 3 + d - 1, at_x(d))
-                         for d in (2, 1, 3)])
-
+        x_copies[group] = [send(sum_c.at[group, x_of(d)], far_x.at[group, d - 1], send_x, recv_x, group * 3 + d - 1, at_x(d))
+                           for d in (2, 1, 3)]
+
+    def second_send(group):
+        for copy in x_copies[group]:
+            copy.wait()
+        total = sum_c[group, x].astype(F32)
+        for d in range(3):
+            total = total + far_x[group, d].astype(F32)
+        sum_x[group] = total.astype(BF)
+        z_copies[group] = [send(sum_x.at[group, z_of(d)], far_z.at[group, d - 1], send_z, recv_z, group * 7 + d - 1, at_z(d))
+                           for d in (4, 3, 5, 2, 6, 1, 7)]
+
+    for h in range(HEADS):
+        for at, grad in ((h * HEAD_DIM, gk_s), (COLS + h * HEAD_DIM, gv_s)):
+            kv_s[:, at:at + HEAD_DIM] = grad[h].astype(BF)
+    for which in range(2):
+        @pl.loop(0, 4)
+        def _(block):
+            lanes = pl.ds(pl.multiple_of(block * 256, 256), 256)
+            value = mm(text_s[:, lanes], kv_s[:, which * COLS:(which + 1) * COLS], TN)
+            put(2 + which, value.astype(BF), block)
+        core_copies[2 + which] = core_send(2 + which)
     frame_term(0, att_s, cot_s)
-    core_copies = [core_send(0)]
+    core_copies[0] = core_send(0)
+    chip_sum(2)
+    chip_sum(3)
     frame_term(1, dq_s, frames_s)
-    core_copies.append(core_send(1))
+    core_copies[1] = core_send(1)
+    chip_sum(0)
+
     for copy in edge_copies:
         copy.wait()
     inner = slice(WINDOW, WINDOW + S_DEV)
@@ -229,63 +273,58 @@
             cols = slice(at, at + HEAD_DIM)
             grad[h, WINDOW:2 * WINDOW] += far_edge[1, :, cols].astype(F32)
             grad[h, S_DEV:WINDOW + S_DEV] += far_edge[0, :, cols].astype(F32)
-            kv_s[:, cols] = grad[h, inner].astype(BF)
-    chip_sum(0)
-
-    for which in range(2):
-        @pl.loop(0, 4)
-        def _(block):
-            lanes = pl.ds(pl.multiple_of(block * 256, 256), 256)
-            value = mm(text_s[inner, lanes], kv_s[:, which * COLS:(which + 1) * COLS], TN)
-            put(2 + which, value.astype(BF), block)
-        core_copies.append(core_send(2 + which))
-    chip_sum(1)
-
+            kv_s[inner, cols] = grad[h, inner].astype(BF)
     for part in range(4):
-        rows = slice(part * 64, part * 64 + 64)
+        rows = slice(WINDOW + part * 64, WINDOW + part * 64 + 64)
         value = mm(kv_s[rows, :COLS], wk_s[...], NT) + mm(kv_s[rows, COLS:], wv_s[...], NT)
         tterm_s[part] = value.astype(BF)
     text_copies = [send(tterm_s.at[y_of(d)], far_t.at[d - 1], send_t, recv_t, d - 1, at_y(d)) for d in (2, 1, 3)]
-    chip_sum(2)
-    chip_sum(3)
-
-    for copy in from_x:
-        copy.wait()
-    from_core = []
-    for d in (1, 2, 3):
-        place = wall_s.at[(head + 4 - d) % 4, core]
-        from_core.append(send(place, place, send_wc, recv_wc, d - 1, at_core))
-
-    z_copies = []
-    for group in range(4):
-        for copy in x_copies[group]:
-            copy.wait()
-        total = sum_c[group, x].astype(F32)
-        for d in range(3):
-            total = total + far_x[group, d].astype(F32)
-        sum_x[group] = total.astype(BF)
-        z_copies.append([send(sum_x.at[group, z_of(d)], far_z.at[group, d - 1], send_z, recv_z, group * 7 + d - 1, at_z(d))
-                         for d in (4, 3, 5, 2, 6, 1, 7)])
-
-    def project(mine_s, far, which, out_s):
-        mine = pl.ds(pl.multiple_of(head * TILE, TILE), TILE)
-        parts = [jnp.transpose(mine_s[:, mine])] + [jnp.transpose(far[d - 1]) for d in (1, 2, 3)]
-        for block in range(4):
-            lanes = slice(block * 256, block * 256 + 256)
-            total = mm(parts[0], wcat_s[which, :, lanes], NN).astype(BF).astype(F32)
-            for d in (1, 2, 3):
-                total = total + mm(parts[d], wall_s[(head + 4 - d) % 4, which, :, lanes], NN).astype(BF).astype(F32)
-            out_s[:, lanes] = total.astype(BF)
-
-    for copy in from_core:
-        copy.wait()
+    chip_sum(1)
+
+    for copy in from_x + from_z:
+        copy.wait()
+    from_core = send(wall_s.at[:, core], wall_s.at[:, core], send_wc, recv_wc, 0, at_core)
+    second_send(2)
+    second_send(3)
+    second_send(0)
+
+    def turned(mine_s, far, d):
+        if d == 0:
+            return jnp.transpose(mine_s[:, pl.ds(pl.multiple_of(head * TILE, TILE), TILE)])
+        return jnp.transpose(far[d - 1])
+
+    def term_of(part, which, d, lanes):
+        weight = wcat_s[which, :, lanes] if d == 0 else wall_s[d - 1, which, :, lanes]
+        return mm(part, weight, NN).astype(BF).astype(F32)
+
+    blocks = [slice(n * 256, n * 256 + 256) for n in range(4)]
+
+    from_core.wait()
     for i in range(6):
         exchange(i, 0).wait()
-    project(att_s, far_att, 0, layer_s)
+    parts = [turned(att_s, far_att, d) for d in range(4)]
+    for lanes in blocks:
+        total = term_of(parts[0], 0, 0, lanes)
+        for d in (1, 2, 3):
+            total = total + term_of(parts[d], 0, d, lanes)
+        layer_s[:, lanes] = total.astype(BF)
     stores = [load(layer_s, layer_hbm, store_sem.at[0])]
-    for i in range(6):
+    second_send(1)
+    for i in (0, 1):
         exchange(i, 1).wait()
-    project(dq_s, far_dq, 1, fgrad_s)
+    parts = [turned(dq_s, far_dq, d) for d in (0, 2)]
+    for lanes in blocks:
+        sum_f[:, lanes] = term_of(parts[0], 1, 0, lanes) + term_of(parts[1], 1, 2, lanes)
+    for i in (2, 4):
+        exchange(i, 1).wait()
+    part = turned(dq_s, far_dq, 1)
+    for lanes in blocks:
+        sum_f[:, lanes] = sum_f[:, lanes] + term_of(part, 1, 1, lanes)
+    for i in (3, 5):
+        exchange(i, 1).wait()
+    part = turned(dq_s, far_dq, 3)
+    for lanes in blocks:
+        fgrad_s[:, lanes] = (sum_f[:, lanes] + term_of(part, 1, 3, lanes)).astype(BF)
     stores.append(load(fgrad_s, fgrad_hbm, store_sem.at[1]))
 
     for copy in text_copies:
@@ -296,7 +335,7 @@
     tgrad_s[...] = total.astype(BF)
     stores.append(load(tgrad_s, tgrad_hbm, store_sem.at[2]))
 
-    for group in range(4):
+    for group in (2, 3, 0, 1):
         for copy in z_copies[group]:
             copy.wait()
         total = sum_x[group, z].astype(F32)
@@ -355,7 +394,7 @@
             pltpu.VMEM((D, COLS), BF),
             pltpu.VMEM((D, COLS), BF),
             pltpu.VMEM((2, COLS, D), BF),
-            pltpu.VMEM((4, 2, COLS, D), BF),
+            pltpu.VMEM((3, 2, COLS, D), BF),
             pltpu.VMEM((HEADS, EXT, HEAD_DIM), BF),
             pltpu.VMEM((HEADS, EXT, HEAD_DIM), BF),
             pltpu.VMEM((COLS, F_DEV), BF),
@@ -369,7 +408,7 @@
             pltpu.VMEM((3, COLS, TILE), BF),
             pltpu.VMEM((2, WINDOW, 2 * COLS), BF),
             pltpu.VMEM((2, WINDOW, 2 * COLS), BF),
-            pltpu.VMEM((S_DEV, 2 * COLS), BF),
+            pltpu.VMEM((EXT, 2 * COLS), BF),
             pltpu.VMEM((4, 2, 4, 8, 16, COLS), BF),
             pltpu.VMEM((4, 4, 8, 16, COLS), BF),
             pltpu.VMEM((4, 4, 8, 16, COLS), BF),
@@ -378,8 +417,9 @@
             pltpu.VMEM((4, 7, 16, COLS), BF),
             pltpu.VMEM((4, 64, D), BF),
             pltpu.VMEM((3, 64, D), BF),
+            pltpu.VMEM((TILE, D), F32),
             dma((5,)), dma((4,)), dma((4,)), dma((4,)),
-            dma((2,)), dma((2,)), dma((3,)), dma((3,)), dma((9,)), dma((9,)), dma((3,)), dma((3,)),
+            dma((2,)), dma((2,)), dma((6,)), dma((6,)), dma((7,)), dma((7,)), dma((3,)), dma((3,)), dma((1,)), dma((1,)),
             dma((6,)), dma((6,)), dma((6,)), dma((6,)), dma((2,)), dma((2,)), dma((4,)), dma((4,)),
             dma((12,)), dma((12,)), dma((28,)), dma((28,)), dma((3,)), dma((3,)),
         ],

time: 57 us -> 54.2 us (0.951)
  Pallas kernels: 56.2 us -> 53.4 us
    pallas_call x1, Pallas kernels: 53.6 us -> 50.9 us  [on_device(): pl.pallas_call(kernel, in_specs=[hbm] * 3 + [vmem] + [hbm] * 4, out_specs...]
where the time goes in v4:
time: 54.2 us; the launch traced here: 54.1 us
  Pallas kernels  53.4 us (99%)
  between operations  0.64 us (1%)
    pallas_call x1, Pallas kernels, on_device(): pl.pallas_call(kernel, in_specs=[hbm] * 3 + [vmem] + [hbm] * 4, out_specs...  50.9 us
    pallas_call x1, Pallas kernels, on_device(): pl.pallas_call(move_kernel, in_specs=[hbm] * 4, out_specs=[hbm] * 7, out_...  2.53 us

profile of v4, /device:TPU:1, one launch (start us, length us, event | category | flops | bytes accessed | tf_op | source)
XLA Modules:
  0.0 54.1 jit_solution(987211638773414150)
XLA Ops:
  0.6 50.9 %shard_map.135 = (bf16[512,1024]{1,0:T(8,128)(2,1)}, bf16[512,1024]{1,0:T(8,128)(2,1)}, bf16[64,1024]{1,0:T(8,128)(2,1)}, f32[4,16,256]{2,1,0:T(8,128)}) custom-call(bf16[2048,1024]{1,0:T(8,128)(2,1)} %frames_hbm.1, bf16[2048,1024]{1,0:T(8,128)(2,1)} %cot_hbm.1, bf16[256,1024]{1,0:T(8,128)(2,1)} %text_hbm.1, s32[1,256]{1,0:T(1,128)} %dur_ref.1, ...), custom_call_target="tpu_custom_call" | custom-call | flops 15000000512 | bytes 16000000 | tf_op jit(solution)/shard_map/pallas_call | solution.py:375
  51.5 2.5 %shard_map.136 = (bf16[512,1024]{1,0:T(8,128)(2,1)}, bf16[512,1024]{1,0:T(8,128)(2,1)}, bf16[64,1024]{1,0:T(8,128)(2,1)}, f32[16,256]{1,0:T(8,128)}, f32[16,256]...) custom-call(bf16[512,1024]{1,0:T(8,128)(2,1)} %get-tuple-element.18.layer_in, ...), custom_call_target="tpu_custom_call" | custom-call | bytes 5000000 | tf_op jit(solution)/shard_map/pallas_call | solution.py:430

commit v5 on v4

--- a/solution.py
+++ b/solution.py
@@ -35,7 +35,7 @@
            layer_s, fgrad_s, tgrad_s, wgrad_s,
            frames_s, cot_s, text_s, wq_s, wk_s, wv_s, wcat_s, wall_s,
            k_s, v_s, qt_s, ut_s, gk_s, gv_s, ends_s, att_s, dq_s,
-           far_att, far_dq, edge_s, far_edge, kv_s, term_s, near_s, sum_c, far_x, sum_x, far_z,
+           far_att, far_dq, edge_s, far_edge, kv_s, term_s, near_s, sum_c, far_x, sum_x, far_z, first_z, sum_z, last_x,
            tterm_s, far_t, sum_f,
            load_w, load_f, load_c, store_sem,
            send_h, recv_h, send_wy, recv_wy, send_wz, recv_wz, send_wx, recv_wx, send_wc, recv_wc,
@@ -185,11 +185,11 @@
         for h in hs:
             att_s[cols[h], rows] = att[h]
         delta = [jnp.sum(u[h].astype(F32) * att[h].astype(F32), axis=0, keepdims=True) for h in hs]
-        ds = [(p[h] * (dp[h] - delta[h]) * HEAD_DIM ** -0.5).astype(BF) for h in hs]
+        ds = [(p[h] * (dp[h] - delta[h])).astype(BF) for h in hs]
         for h in hs:
             gv_s[h, here, :] += mm(pb[h], u[h], NT)
         for h in hs:
-            dq_s[cols[h], rows] = mm(k[h], ds[h], TN).astype(BF)
+            dq_s[cols[h], rows] = (mm(k[h], ds[h], TN) * HEAD_DIM ** -0.5).astype(BF)
         for h in hs:
             gk_s[h, here, :] += mm(ds[h], q[h], NT)
 
@@ -197,6 +197,7 @@
         def _():
             exchange(i, 0).start()
 
+    gk_s[...] = gk_s[...] * HEAD_DIM ** -0.5
     for h in range(HEADS):
         cols = slice(h * HEAD_DIM, (h + 1) * HEAD_DIM)
         later = slice(COLS + h * HEAD_DIM, COLS + (h + 1) * HEAD_DIM)
@@ -210,16 +211,17 @@
         exchange(i, 1).start()
 
     def put(group, value, block):
-        for part in range(2):
+        parts = value.shape[0] // 128
+        for part in range(parts):
             for chip in range(4):
                 for side in range(2):
                     at = part * 128 + chip * 32 + side * 16
-                    term_s[group, side, chip, block * 2 + part, :, :] = value[at:at + 16]
+                    term_s[group, side, chip, block * parts + part, :, :] = value[at:at + 16]
 
     def frame_term(group, left_s, right_s):
-        @pl.loop(0, 4)
+        @pl.loop(0, 2)
         def _(block):
-            lanes = pl.ds(pl.multiple_of(block * 256, 256), 256)
+            lanes = pl.ds(pl.multiple_of(block * 512, 512), 512)
             value = mm(left_s[...], right_s[:, lanes], NN)
             put(group, jnp.transpose(value).astype(BF), block)
 
@@ -234,10 +236,23 @@
         @pl.loop(0, 4)
         def _(chip):
             sum_c[group, chip] = (term_s[group, core, chip].astype(F32) + near_s[group, chip].astype(F32)).astype(BF)
+        if group == 1:
+            z_copies[group] = [send(sum_c.at[group, :, z_of(d)], first_z.at[d - 1], send_z, recv_z, group * 7 + d - 1, at_z(d))
+                               for d in (4, 3, 5, 2, 6, 1, 7)]
+            return
         x_copies[group] = [send(sum_c.at[group, x_of(d)], far_x.at[group, d - 1], send_x, recv_x, group * 3 + d - 1, at_x(d))
                            for d in (2, 1, 3)]
 
     def second_send(group):
+        if group == 1:
+            for copy in z_copies[group]:
+                copy.wait()
+            total = sum_c[group, :, z].astype(F32)
+            for d in range(7):
+                total = total + first_z[d].astype(F32)
+            sum_z[...] = total.astype(BF)
+            x_copies[group] = [send(sum_z.at[x_of(d)], last_x.at[d - 1], send_x, recv_x, group * 3 + d - 1, at_x(d)) for d in (2, 1, 3)]
+            return
         for copy in x_copies[group]:
             copy.wait()
         total = sum_c[group, x].astype(F32)
@@ -250,13 +265,14 @@
     for h in range(HEADS):
         for at, grad in ((h * HEAD_DIM, gk_s), (COLS + h * HEAD_DIM, gv_s)):
             kv_s[:, at:at + HEAD_DIM] = grad[h].astype(BF)
-    for which in range(2):
-        @pl.loop(0, 4)
-        def _(block):
-            lanes = pl.ds(pl.multiple_of(block * 256, 256), 256)
-            value = mm(text_s[:, lanes], kv_s[:, which * COLS:(which + 1) * COLS], TN)
-            put(2 + which, value.astype(BF), block)
-        core_copies[2 + which] = core_send(2 + which)
+    @pl.loop(0, 4)
+    def _(block):
+        lanes = pl.ds(pl.multiple_of(block * 256, 256), 256)
+        value = mm(text_s[:, lanes], kv_s[...], TN).astype(BF)
+        put(2, value[:, :COLS], block)
+        put(3, value[:, COLS:], block)
+    core_copies[2] = core_send(2)
+    core_copies[3] = core_send(3)
     frame_term(0, att_s, cot_s)
     core_copies[0] = core_send(0)
     chip_sum(2)
@@ -335,13 +351,19 @@
     tgrad_s[...] = total.astype(BF)
     stores.append(load(tgrad_s, tgrad_hbm, store_sem.at[2]))
 
-    for group in (2, 3, 0, 1):
+    for group in (2, 3, 0):
         for copy in z_copies[group]:
             copy.wait()
         total = sum_x[group, z].astype(F32)
         for d in range(7):
             total = total + far_z[group, d].astype(F32)
         wgrad_s[group] = total
+    for copy in x_copies[1]:
+        copy.wait()
+    total = sum_z[x].astype(F32)
+    for d in range(3):
+        total = total + last_x[d].astype(F32)
+    wgrad_s[1] = total
     stores.append(load(wgrad_s, wgrad_hbm, store_sem.at[3]))
     for copy in stores:
         copy.wait()
@@ -415,6 +437,9 @@
             pltpu.VMEM((4, 3, 8, 16, COLS), BF),
             pltpu.VMEM((4, 8, 16, COLS), BF),
             pltpu.VMEM((4, 7, 16, COLS), BF),
+            pltpu.VMEM((7, 4, 16, COLS), BF),
+            pltpu.VMEM((4, 16, COLS), BF),
+            pltpu.VMEM((3, 16, COLS), BF),
             pltpu.VMEM((4, 64, D), BF),
             pltpu.VMEM((3, 64, D), BF),
             pltpu.VMEM((TILE, D), F32),

time: 54.2 us -> 55.1 us (1.017)
  Pallas kernels: 53.4 us -> 54.3 us
    pallas_call x1, Pallas kernels: 50.9 us -> 51.7 us  [on_device(): pl.pallas_call(kernel, in_specs=[hbm] * 3 + [vmem] + [hbm] * 4, out_specs...]
where the time goes in v5:
time: 55.1 us; the launch traced here: 54.9 us
  Pallas kernels  54.3 us (99%)
  between operations  0.64 us (1%)
    pallas_call x1, Pallas kernels, on_device(): pl.pallas_call(kernel, in_specs=[hbm] * 3 + [vmem] + [hbm] * 4, out_specs...  51.7 us
    pallas_call x1, Pallas kernels, on_device(): pl.pallas_call(move_kernel, in_specs=[hbm] * 4, out_specs=[hbm] * 7, out_...  2.53 us

profile of v5, /device:TPU:1, one launch (start us, length us, event | category | flops | bytes accessed | tf_op | source)
XLA Modules:
  0.0 54.9 jit_solution(15369037069192040552)
XLA Ops:
  0.6 51.7 %shard_map.135 = (bf16[512,1024]{1,0:T(8,128)(2,1)}, bf16[512,1024]{1,0:T(8,128)(2,1)}, bf16[64,1024]{1,0:T(8,128)(2,1)}, f32[4,16,256]{2,1,0:T(8,128)}) custom-call(bf16[2048,1024]{1,0:T(8,128)(2,1)} %frames_hbm.1, bf16[2048,1024]{1,0:T(8,128)(2,1)} %cot_hbm.1, bf16[256,1024]{1,0:T(8,128)(2,1)} %text_hbm.1, s32[1,256]{1,0:T(1,128)} %dur_ref.1, ...), custom_call_target="tpu_custom_call" | custom-call | flops 15000000512 | bytes 16000000 | tf_op jit(solution)/shard_map/pallas_call | solution.py:397
  52.4 2.5 %shard_map.136 = (bf16[512,1024]{1,0:T(8,128)(2,1)}, bf16[512,1024]{1,0:T(8,128)(2,1)}, bf16[64,1024]{1,0:T(8,128)(2,1)}, f32[16,256]{1,0:T(8,128)}, f32[16,256]...) custom-call(bf16[512,1024]{1,0:T(8,128)(2,1)} %get-tuple-element.18.layer_in, ...), custom_call_target="tpu_custom_call" | custom-call | bytes 5000000 | tf_op jit(solution)/shard_map/pallas_call | solution.py:455
